TPU v7x, 512 devices: a whole 4x8x8 slice. The times are simulated.
512 devices in a mesh: gx: 64 (over y_lo, z, core), ha: 8 (over y_hi, x).
Axes of the slice: x: 4, y: 8 (y_hi: 2, y_lo: 4; y = y_hi * 4 + y_lo), z: 8, core: 2. Of those that a mesh axis runs over, the one named last changes fastest.
Arguments:
- wall_history: bfloat16 [3, 3, 8192, 1024], P(None, None, 'gx', 'ha'), may hold values from -6 to 6
- kernel_taps: bfloat16 [8, 3, 3, 257], P('ha'), may hold values from -0.125 to 0.125
- span_gains: float32 [8, 9], P('ha'), may hold values from -2 to 2
Outputs:
- velocity: float32 [8, 8192, 1024], P('ha', 'gx')
All inputs are finite; a program needn't handle non-finite values.
Results may differ from a plain program's by a relative error of at most 0.0003.
Values may be sent and summed in bfloat16 or wider, within the bound.
No kernel may reach another device: no remote copies, remote signals or barrier semaphores. Data moves between devices by JAX's collectives and lax.ppermute only.
A program may use at most 64 MiB of HBM per device.

v0:
```python
import jax
import jax.numpy as jnp
from jax import lax
from jax.sharding import PartitionSpec as P


def padded_2(cells, sides, width):
    for axis, dim in sides:
        count = lax.axis_size(axis)
        head = lax.slice_in_dim(cells, 0, width, axis=dim)
        tail = lax.slice_in_dim(cells, cells.shape[dim] - width, cells.shape[dim], axis=dim)
        cells = jnp.concatenate(
            [
                lax.ppermute(tail, axis, [(i, (i + 1) % count) for i in range(count)]),
                cells,
                lax.ppermute(head, axis, [((i + 1) % count, i) for i in range(count)]),
            ],
            axis=dim,
        )
    return cells


def banded(taps, window):
    count = window - taps.shape[-1] + 1
    padded = jnp.concatenate([taps, jnp.zeros(taps.shape[:-1] + (count,), taps.dtype)], axis=-1)
    tiled = jnp.tile(padded, count)[..., : count * window]
    return tiled.reshape(taps.shape[:-1] + (count, window))


def streamwise(kernels, extended):
    window = extended.shape[2]

    def one_height(taps):
        band = banded(taps, window)
        return jnp.einsum("scxw,scwz->xz", band, extended, preferred_element_type=jnp.float32)

    return lax.map(one_height, kernels)


def spanwise(read, gains):
    span_taps = gains.shape[1]
    half = (span_taps - 1) // 2
    result = jnp.zeros(read.shape, jnp.float32)
    for shift in range(span_taps):
        result = result + gains[:, shift][:, None, None] * jnp.roll(read, half - shift, axis=2)
    return result


def local(wall_history, kernel_taps, span_gains):
    reach = (kernel_taps.shape[-1] - 1) // 2
    planes = lax.all_gather(wall_history, "ha", axis=3, tiled=True)
    extended = padded_2(planes, (("gx", 2),), reach)
    velocity = spanwise(streamwise(kernel_taps, extended), span_gains)
    return velocity


def solution(mesh):
    in_specs = (P(None, None, "gx", "ha"), P("ha", None, None, None), P("ha", None))
    out_specs = P("ha", "gx", None)
    return jax.shard_map(local, mesh=mesh, in_specs=in_specs, out_specs=out_specs, check_vma=False)
```

profile of v0, /device:TPU:16, one launch (start us, length us, event | category | flops | bytes accessed | tf_op | source)
XLA Modules:
  0.0 156.5 jit_solution(3926553398121521910)
XLA Ops:
  6.5 0.0 all-gather.2.cloned.1.call-start
  6.5 1.7 %copy.9 = bf16[3,3,128,128]{3,2,0,1:T(8,128)(2,1)} copy(bf16[3,3,128,128]{3,2,1,0:T(8,128)(2,1)} %param.3) | data formatting | bytes 589824 | tf_op args[0]
  8.2 0.0 all-gather.2.cloned.1.call-update
  8.3 90.6 %all-gather.2.cloned.1.call-done = bf16[3,3,128,1024]{3,2,0,1:T(8,128)(2,1)} async-done(((bf16[3,3,128,128]{3,2,0,1:T(8,128)(2,1)}), bf16[3,3,128,1024]{3,2,0,1:T(8,128)(2,1)}) %all-gather.2.cloned.1.call-update) | async-done | bytes 2359312 | tf_op jit(solution)/shard_map/all_gather | solution.py:51
  98.9 6.1 %collective-permute-start.1 = (bf16[3,3,128,1024]{3,2,0,1:T(8,128)(2,1)}, bf16[3,3,128,1024]{3,2,0,1:T(8,128)(2,1)}, u32[]{:S(2)}, u32[]{:S(2)}) collective-permute-start(bf16[3,3,128,1024]{3,2,0,1:T(8,128)(2,1)} %all-gather.2.cloned.1.call-done), channel_id=1, source_target_pairs={{8,0},{16,8},{24,16},{32,24},{40,32},{48,40},{56,48},{64,56},{72,6... | collective-permute-start | bytes 7077896 | tf_op jit(solution)/shard_map/ppermute | solution.py:16
  105.0 1.9 %collective-permute-start = (bf16[3,3,128,1024]{3,2,0,1:T(8,128)(2,1)}, bf16[3,3,128,1024]{3,2,0,1:T(8,128)(2,1)}, u32[]{:S(2)}, u32[]{:S(2)}) collective-permute-start(bf16[3,3,128,1024]{3,2,0,1:T(8,128)(2,1)} %all-gather.2.cloned.1.call-done), channel_id=1, source_target_pairs={{0,8},{8,16},{16,24},{24,32},{32,40},{40,48},{48,56},{56,64},{64,7... | collective-permute-start | bytes 7077896 | tf_op jit(solution)/shard_map/ppermute | solution.py:14
  106.9 0.7 concatenate.79
  107.6 0.1 tile.14
  107.7 2.9 %tile.15 = bf16[3,3,49280]{2,1,0:T(4,128)(2,1)S(1)} reshape(bf16[3,3,128,385]{3,2,1,0:T(8,128)(2,1)S(1)} %tile.14) | data formatting | bytes 1774080 | tf_op jit(solution)/shard_map/while/body/eval_jaxpr/tile | solution.py:26
  110.6 0.0 copy-start
  110.6 0.4 slice.121
  111.0 1.3 reshape.70
  112.3 0.0 copy-done
  112.3 0.7 fusion.17
  113.0 18.7 %collective-permute-done.1 = bf16[3,3,128,1024]{3,2,0,1:T(8,128)(2,1)} collective-permute-done((bf16[3,3,128,1024]{3,2,0,1:T(8,128)(2,1)}, bf16[3,3,128,1024]{3,2,0,1:T(8,128)(2,1)}, u32[]{:S(2)}, u32[]{:S(2)}) %collective-permute-start.1) | collective-permute-done | bytes 2359328 | tf_op jit(solution)/shard_map/ppermute | solution.py:16
  131.6 5.9 %collective-permute-done = bf16[3,3,128,1024]{3,2,0,1:T(8,128)(2,1)} collective-permute-done((bf16[3,3,128,1024]{3,2,0,1:T(8,128)(2,1)}, bf16[3,3,128,1024]{3,2,0,1:T(8,128)(2,1)}, u32[]{:S(2)}, u32[]{:S(2)}) %collective-permute-start) | collective-permute-done | bytes 2359328 | tf_op jit(solution)/shard_map/ppermute | solution.py:14
  137.6 3.8 %fusion = f32[128,1024,1,1]{1,0,3,2:T(8,128)S(1)} fusion(bf16[3,3,128,1024]{3,2,0,1:T(8,128)(2,1)} %collective-permute-done.1, bf16[3,3,128,1024]{3,2,0,1:T(8,128)(2,1)} %all-gather.2.cloned.1.call-done, bf16[3,3,128,1024]{3,2,0,1:T(8,128)(2,1)} %collective-permute-done, bf16[3,3,128,384]{3,2,1,0:T(8,128)(2,1)S(1)} %reshape.70), kind=kOutput, calls=%fused_computation | convolution fusion | flops 927203328 | bytes 8486912 | tf_op jit(solution)/shard_map/while/body/eval_jaxpr/scxw,scwz->xz/dot_general | solution.py:35
  141.4 0.1 slice_bitcast_fusion.11
  141.4 0.1 slice_bitcast_fusion.10
  141.5 0.1 slice_bitcast_fusion.9
  141.6 0.1 slice_bitcast_fusion.8
  141.7 0.2 slice_bitcast_fusion.3
  141.9 0.2 slice_bitcast_fusion.2
  142.1 0.2 slice_bitcast_fusion.1
  142.3 0.2 slice_bitcast_fusion
  142.5 7.1 %fusion.15 = f32[1,128,1024]{2,1,0:T(8,128)} fusion(f32[128,1020]{1,0:T(8,128)S(1)} %get-tuple-element.16, f32[128,4]{1,0:T(8,128)S(1)} %get-tuple-element.20, f32[128,1021]{1,0:T(8,128)S(1)} %get-tuple-element.22, f32[128,3]{1,0:T(8,128)S(1)} %get-tuple-element.24, f32[128,1022]{1,0:T(8,128)S(1)} %get-tuple-element.26, f32[128,2]{1,0:T(8,128)S(1)} %get-tuple-element.28, ...), kind=kLoop, calls=%fused_computation.24 | loop fusion | flops 3276800 | bytes 5242916 | tf_op jit(solution)/shard_map/add | solution.py:45
Async XLA Ops:
  6.5 92.4 %all-gather.2.cloned.1.call-start = ((), (), s32[]{:S(2)}) async-start(), calls=%async_computation | async-start | bytes 2654208 | tf_op jit(solution)/shard_map/all_gather | solution.py:51
  98.9 32.7 %collective-permute-start.1 = (bf16[3,3,128,1024]{3,2,0,1:T(8,128)(2,1)}, bf16[3,3,128,1024]{3,2,0,1:T(8,128)(2,1)}, u32[]{:S(2)}, u32[]{:S(2)}) collective-permute-start(bf16[3,3,128,1024]{3,2,0,1:T(8,128)(2,1)} %all-gather.2.cloned.1.call-done), channel_id=1, source_target_pairs={{8,0},{16,8},{24,16},{32,24},{40,32},{48,40},{56,48},{64,56},{72,6... | collective-permute-start | bytes 7077896 | tf_op jit(solution)/shard_map/ppermute | solution.py:16
  105.0 32.6 %collective-permute-start = (bf16[3,3,128,1024]{3,2,0,1:T(8,128)(2,1)}, bf16[3,3,128,1024]{3,2,0,1:T(8,128)(2,1)}, u32[]{:S(2)}, u32[]{:S(2)}) collective-permute-start(bf16[3,3,128,1024]{3,2,0,1:T(8,128)(2,1)} %all-gather.2.cloned.1.call-done), channel_id=1, source_target_pairs={{0,8},{8,16},{16,24},{24,32},{32,40},{40,48},{48,56},{56,64},{64,7... | collective-permute-start | bytes 7077896 | tf_op jit(solution)/shard_map/ppermute | solution.py:14
  110.6 1.7 %copy-start = (f32[1,9]{1,0:T(1,128)S(1)}, f32[1,9]{1,0:T(1,128)}, u32[]{:S(2)}) copy-start(f32[1,9]{1,0:T(1,128)} %param.5) | copy-start | bytes 112
Sparse Core Ops, SparseCore 0:
  10.4 88.4 all-gather.1
where the time goes:
time: 157 us; the launch traced here: 156 us
  waiting for transfers between devices  115 us (73%)
  between operations  13.5 us (9%)
  local copies, waits for them, and re-layouts  8.87 us (6%)
  starting transfers between devices  8.01 us (5%)
  other arithmetic  7.1 us (5%)
  matrix products  3.77 us (2%)
    all_gather x1, waiting for transfers between devices, local(): planes = lax.all_gather(wall_history, 'ha', axis=3, tiled=True)  90.6 us
    ppermute x1, waiting for transfers between devices, padded_2(): lax.ppermute(head, axis, [((i + 1) % count, i) for i in range(count)])  18.7 us
    add x1, other arithmetic, spanwise(): result + gains[:, shift][:, None, None] * jnp.roll(read, half - shift, ax...  7.1 us
    ppermute x1, starting transfers between devices, padded_2(): lax.ppermute(head, axis, [((i + 1) % count, i) for i in range(count)])  6.08 us
    ppermute x1, waiting for transfers between devices, padded_2(): lax.ppermute(tail, axis, [(i, (i + 1) % count) for i in range(count)])  5.93 us
    dot_general x1, matrix products, one_height(): jnp.einsum('scxw,scwz->xz', band, extended, preferred_element_type=jnp.fl...  3.77 us
  transfers between devices with their start and end apart: 3, of which 3 were waited for; matrix products, arithmetic and copies ran while one was open for 4% of the time, Pallas kernels for 0%

commit v1 on v0

v1 whole, which is shorter than its diff:
```python
import jax
import jax.numpy as jnp
from jax import lax
from jax.experimental import pallas as pl
from jax.experimental.pallas import tpu as pltpu
from jax.sharding import PartitionSpec as P

SUB = 32


def band_kernel(parity_ref, rows_ref, own_ref, near_ref, far_ref, read_ref, band_ref):
    planes, cells, width = own_ref.shape
    heights = rows_ref.shape[0]
    depth = rows_ref.shape[1]
    window = 2 * cells + SUB
    for h in range(heights):
        row = jnp.broadcast_to(rows_ref[pl.ds(h, 1), :], (SUB, depth))
        band_ref[pl.ds(h * SUB, SUB), :] = pltpu.roll(row, 0, 1, stride=1, stride_axis=0).astype(jnp.bfloat16)
    even = parity_ref[0] == 0
    near, far = near_ref[...], far_ref[...]
    before = jnp.where(even, far, near)
    after = jnp.where(even, near, far)
    for b in range(cells // SUB):
        pieces = []
        for c in range(planes):
            pieces += [before[c, b * SUB :, :], own_ref[c], after[c, : (b + 1) * SUB, :]]
        pieces.append(jnp.zeros((depth - planes * window, width), jnp.bfloat16))
        span = jnp.concatenate(pieces, axis=0)
        part = jnp.dot(band_ref[...], span, preferred_element_type=jnp.float32)
        for h in range(heights):
            read_ref[h, pl.ds(b * SUB, SUB), :] = part[h * SUB : (h + 1) * SUB, :]


def span_kernel(gains_ref, read_ref, velocity_ref):
    blocks = read_ref.shape[0]
    taps = gains_ref.shape[1]
    half = (taps - 1) // 2
    read = jnp.concatenate([read_ref[j] for j in range(blocks)], axis=1)
    total = gains_ref[0, half] * read
    for e in range(taps):
        if e != half:
            total = total + gains_ref[0, e] * pltpu.roll(read, (half - e) % read.shape[1], 1)
    velocity_ref[0] = total


def local(wall_history, kernel_taps, span_gains):
    snaps, chans, cells, width = wall_history.shape
    taps = kernel_taps.shape[-1]
    planes = snaps * chans
    window = taps - 1 + SUB
    groups = lax.axis_size("ha")
    count = lax.axis_size("gx")
    depth = -(-planes * window // 128) * 128
    own = wall_history.reshape(planes, cells, width)
    far = lax.ppermute(own, "gx", [(i, (i - 1 if i % 2 == 0 else i + 1) % count) for i in range(count)])
    near = lax.ppermute(own, "gx", [(i, i ^ 1) for i in range(count)])
    rows = jnp.pad(kernel_taps.astype(jnp.float32).reshape(planes, taps), ((0, 0), (0, window - taps))).reshape(1, planes * window)
    rows = jnp.pad(rows, ((0, 0), (0, depth - planes * window)))
    rows = lax.all_to_all(jnp.broadcast_to(rows, (groups, depth)), "ha", 0, 0, tiled=True)
    parity = (lax.axis_index("gx") % 2).astype(jnp.int32).reshape(1)
    read = pl.pallas_call(
        band_kernel,
        out_shape=jax.ShapeDtypeStruct((groups, cells, width), jnp.float32),
        in_specs=[pl.BlockSpec(memory_space=pltpu.SMEM)] + [pl.BlockSpec(memory_space=pltpu.VMEM)] * 4,
        out_specs=pl.BlockSpec(memory_space=pltpu.VMEM),
        scratch_shapes=[pltpu.VMEM((groups * SUB, depth), jnp.bfloat16)],
        compiler_params=pltpu.CompilerParams(vmem_limit_bytes=32 * 1024 * 1024),
        cost_estimate=pl.CostEstimate(flops=2 * groups * cells * width * planes * window, bytes_accessed=2 << 20, transcendentals=0),
    )(parity, rows, own, near, far)
    read = lax.all_to_all(read, "ha", 0, 0, tiled=True)
    block = 32
    return pl.pallas_call(
        span_kernel,
        grid=(cells // block,),
        out_shape=jax.ShapeDtypeStruct((1, cells, groups * width), jnp.float32),
        in_specs=[pl.BlockSpec(memory_space=pltpu.SMEM), pl.BlockSpec((groups, block, width), lambda i: (0, i, 0))],
        out_specs=pl.BlockSpec((1, block, groups * width), lambda i: (0, i, 0)),
        compiler_params=pltpu.CompilerParams(vmem_limit_bytes=32 * 1024 * 1024),
    )(span_gains, read)


def solution(mesh):
    in_specs = (P(None, None, "gx", "ha"), P("ha", None, None, None), P("ha", None))
    out_specs = P("ha", "gx", None)
    return jax.shard_map(local, mesh=mesh, in_specs=in_specs, out_specs=out_specs, check_vma=False)
```

time: 157 us -> 60.3 us (0.38)
  the two profiles are of different devices: /device:TPU:16 before, /device:TPU:8 now
where the time goes in v1:
time: 60.3 us; the launch traced here: 59.9 us
  starting transfers between devices  21.9 us (36%)
  blocking collectives  20.8 us (34%)
  waiting for transfers between devices  10.9 us (18%)
  Pallas kernels  4.66 us (8%)
  local copies, waits for them, and re-layouts  1.52 us (3%)
    all_to_all x1, blocking collectives, local(): read = lax.all_to_all(read, 'ha', 0, 0, tiled=True)  20.8 us
    all_to_all x1, waiting for transfers between devices, local(): lax.all_to_all(jnp.broadcast_to(rows, (groups, depth)), 'ha', 0, 0, tiled...  10.9 us
    ppermute x1, starting transfers between devices, local(): lax.ppermute(own, 'gx', [(i, (i - 1 if i % 2 == 0 else i + 1) % count) fo...  10.4 us
    all_to_all x1, starting transfers between devices, local(): lax.all_to_all(jnp.broadcast_to(rows, (groups, depth)), 'ha', 0, 0, tiled...  9.56 us
    pallas_call x1, Pallas kernels, local(): pl.pallas_call(span_kernel, grid=(cells // block,), out_shape=jax.ShapeDt...  2.94 us
    ppermute x1, starting transfers between devices, local(): near = lax.ppermute(own, 'gx', [(i, i ^ 1) for i in range(count)])  1.92 us
    pallas_call x1, Pallas kernels, local(): pl.pallas_call(band_kernel, out_shape=jax.ShapeDtypeStruct((groups, cells...  1.72 us
  transfers between devices with their start and end apart: 3, of which 1 were waited for; matrix products, arithmetic and copies ran while one was open for 3% of the time, Pallas kernels for 0%

profile of v1, /device:TPU:8, one launch (start us, length us, event | category | flops | bytes accessed | tf_op | source)
XLA Modules:
  0.0 59.9 jit_solution(13309740014608468856)
XLA Ops:
  0.0 0.0 copy-start.1
  0.0 10.4 %collective-permute-start.1 = (bf16[9,128,128]{2,1,0:T(8,128)(2,1)}, bf16[9,128,128]{2,1,0:T(8,128)(2,1)S(1)}, u32[]{:S(2)}, u32[]{:S(2)}) collective-permute-start(bf16[9,128,128]{2,1,0:T(8,128)(2,1)} %bitcast.6), channel_id=1, source_target_pairs={{0,504},{8,16},{16,8},{24,32},{32,24},{40,48},{48,40},{56,64},{64,... | collective-permute-start | bytes 884744 | tf_op jit(solution)/shard_map/ppermute | solution.py:55
  10.4 1.9 %collective-permute-start = (bf16[9,128,128]{2,1,0:T(8,128)(2,1)}, bf16[9,128,128]{2,1,0:T(8,128)(2,1)S(1)}, u32[]{:S(2)}, u32[]{:S(2)}) collective-permute-start(bf16[9,128,128]{2,1,0:T(8,128)(2,1)} %bitcast.7), channel_id=1, source_target_pairs={{0,8},{8,0},{16,24},{24,16},{32,40},{40,32},{48,56},{56,48},{64,72... | collective-permute-start | bytes 884744 | tf_op jit(solution)/shard_map/ppermute | solution.py:56
  12.3 0.7 %reshape.22 = bf16[9,257]{1,0:T(8,128)(2,1)S(1)} reshape(bf16[1,3,3,257]{3,2,1,0:T(4,128)(2,1)} %param.4) | data formatting | bytes 9252 | tf_op jit(solution)/shard_map/reshape | solution.py:57
  13.1 0.1 reshape.23
  13.2 0.7 %broadcast_in_dim.2 = f32[8,1,2688]{2,1,0:T(1,128)} broadcast(f32[2688]{0:T(1024)S(1)} %convert_reduce_fusion), dimensions={2} | broadcast | bytes 96768 | tf_op jit(solution)/shard_map/broadcast_in_dim | solution.py:59
  13.9 9.6 %all-to-all-start = ((f32[8,1,2688]{2,1,0:T(1,128)}), f32[8,1,2688]{2,1,0:T(1,128)S(1)}, u32[]{:S(2)}, u32[]{:S(2)}) async-start(f32[8,1,2688]{2,1,0:T(1,128)} %broadcast_in_dim.2), calls=%async_computation | async-start | bytes 172032 | tf_op jit(solution)/shard_map/all_to_all | solution.py:59
  23.5 10.9 %all-to-all-done = f32[8,1,2688]{2,1,0:T(1,128)S(1)} async-done(((f32[8,1,2688]{2,1,0:T(1,128)}), f32[8,1,2688]{2,1,0:T(1,128)S(1)}, u32[]{:S(2)}, u32[]{:S(2)}) %all-to-all-start) | async-done | bytes 86048 | tf_op jit(solution)/shard_map/all_to_all | solution.py:59
  34.4 0.0 collective-permute-done.1.far_ref
  34.4 0.0 collective-permute-done.near_ref
  34.4 0.0 copy-done.1
  34.4 1.7 %shard_map.37 = f32[8,128,128]{2,1,0:T(8,128)S(1)} custom-call(s32[1]{0:T(128)} %bitcast.parity_ref, f32[8,2688]{1,0:T(8,128)S(1)} %bitcast.5, bf16[9,128,128]{2,1,0:T(8,128)(2,1)S(1)} %bitcast.8, bf16[9,128,128]{2,1,0:T(8,128)(2,1)S(1)} %collective-permute-done.near_ref, bf16[9,128,128]{2,1,0:T(8,128)(2,1)S(1)} %collective-permute-done.1.far_ref), custom_call_target="tpu_custom_call" | custom-call | flops 679477248 | bytes 2097152 | tf_op jit(solution)/shard_map/pallas_call | solution.py:61
  36.2 0.0 copy-start
  36.2 20.8 %all_to_all.13.read_ref = f32[8,128,128]{2,1,0:T(8,128)S(1)} all-to-all(f32[8,128,128]{2,1,0:T(8,128)S(1)} %shard_map.37), channel_id=1, replica_groups=mesh['gx'=64,'ha'=8] {'ha'}, dimensions={0} | all-to-all | bytes 1048576 | tf_op jit(solution)/shard_map/all_to_all | solution.py:70
  57.0 0.0 copy-done
  57.0 2.9 %shard_map.38 = f32[1,128,1024]{2,1,0:T(8,128)} custom-call(f32[1,9]{1,0:T(1,128)S(1)} %copy-done, f32[8,128,128]{2,1,0:T(8,128)S(1)} %all_to_all.13.read_ref), custom_call_target="tpu_custom_call" | custom-call | tf_op jit(solution)/shard_map/pallas_call | solution.py:72
  (3 shorter events, 0.1 us)
Async XLA Ops:
  0.0 34.4 %copy-start.1 = (bf16[3,3,128,128]{3,2,1,0:T(8,128)(2,1)S(1)}, bf16[3,3,128,128]{3,2,1,0:T(8,128)(2,1)}, u32[]{:S(2)}) copy-start(bf16[3,3,128,128]{3,2,1,0:T(8,128)(2,1)} %param.3) | copy-start | bytes 884740
  0.0 34.4 %collective-permute-start.1 = (bf16[9,128,128]{2,1,0:T(8,128)(2,1)}, bf16[9,128,128]{2,1,0:T(8,128)(2,1)S(1)}, u32[]{:S(2)}, u32[]{:S(2)}) collective-permute-start(bf16[9,128,128]{2,1,0:T(8,128)(2,1)} %bitcast.6), channel_id=1, source_target_pairs={{0,504},{8,16},{16,8},{24,32},{32,24},{40,48},{48,40},{56,64},{64,... | collective-permute-start | bytes 884744 | tf_op jit(solution)/shard_map/ppermute | solution.py:55
  10.4 24.0 %collective-permute-start = (bf16[9,128,128]{2,1,0:T(8,128)(2,1)}, bf16[9,128,128]{2,1,0:T(8,128)(2,1)S(1)}, u32[]{:S(2)}, u32[]{:S(2)}) collective-permute-start(bf16[9,128,128]{2,1,0:T(8,128)(2,1)} %bitcast.7), channel_id=1, source_target_pairs={{0,8},{8,0},{16,24},{24,16},{32,40},{40,32},{48,56},{56,48},{64,72... | collective-permute-start | bytes 884744 | tf_op jit(solution)/shard_map/ppermute | solution.py:56
  13.9 20.5 %all-to-all-start = ((f32[8,1,2688]{2,1,0:T(1,128)}), f32[8,1,2688]{2,1,0:T(1,128)S(1)}, u32[]{:S(2)}, u32[]{:S(2)}) async-start(f32[8,1,2688]{2,1,0:T(1,128)} %broadcast_in_dim.2), calls=%async_computation | async-start | bytes 172032 | tf_op jit(solution)/shard_map/all_to_all | solution.py:59
  36.2 20.8 %copy-start = (f32[1,9]{1,0:T(1,128)S(1)}, f32[1,9]{1,0:T(1,128)}, u32[]{:S(2)}) copy-start(f32[1,9]{1,0:T(1,128)} %gains_ref.1) | copy-start | bytes 112

commit v2 on v1

v2 whole, which is shorter than its diff:
```python
import jax
import jax.numpy as jnp
from jax import lax
from jax.experimental import pallas as pl
from jax.experimental.pallas import tpu as pltpu
from jax.sharding import PartitionSpec as P

SUB = 32
NOTES = 16
LEVELS = 30719.0
OFFSET = 120.0
LOG2E = 1.4426950408889634
TINY = 1.2e-38


def row_kernel(taps_ref, rows_ref):
    groups, _, depth = rows_ref.shape
    snaps, chans, taps = taps_ref.shape
    pieces = []
    for s in range(snaps):
        for c in range(chans):
            pieces += [taps_ref[s, c : c + 1, :].astype(jnp.float32), jnp.zeros((1, SUB - 1), jnp.float32)]
    pieces.append(jnp.zeros((1, depth - snaps * chans * (taps + SUB - 1)), jnp.float32))
    row = jnp.concatenate(pieces, axis=1)
    for h in range(groups):
        rows_ref[h] = row


def gains_kernel(gains_ref, wide_ref):
    for e in range(gains_ref.shape[1]):
        wide_ref[e] = jnp.broadcast_to(gains_ref[0:1, e : e + 1], wide_ref.shape[1:])


def band_kernel(rows_ref, band_ref):
    heights, _, depth = rows_ref.shape
    for h in range(heights):
        row = jnp.broadcast_to(rows_ref[h], (SUB, depth))
        band_ref[pl.ds(h * SUB, SUB), :] = pltpu.roll(row, 0, 1, stride=1, stride_axis=0).astype(jnp.bfloat16)


def coded(values):
    peak = jnp.max(jnp.abs(values), axis=0, keepdims=True) * (1 + 1 / 128)
    scale = jnp.maximum(peak.astype(jnp.bfloat16).astype(jnp.float32), TINY)
    level = jnp.floor(jnp.abs(values) * (1.0 / scale) * LEVELS + 0.5) * (1 / 128)
    octave = jnp.floor(level)
    size = (level - octave + 1.0) * jnp.exp2(octave - OFFSET)
    return jnp.where(values < 0, -size, size).astype(jnp.bfloat16), scale


def decoded(code, scale):
    code = code.astype(jnp.float32)
    size = jnp.abs(code)
    octave = jnp.floor(jnp.log(size) * LOG2E)
    level = (octave + (OFFSET - 1.0) + size * jnp.exp2(-octave)) * (scale * (128 / LEVELS))
    return jnp.where(code < 0, -level, level)


def read_kernel(even_ref, band_ref, own_ref, near_ref, far_ref, read_ref):
    planes, cells, width = own_ref.shape
    heights = read_ref.shape[0]
    depth = band_ref.shape[1]
    window = 2 * cells + SUB
    even = even_ref[0] == 1
    near, far = near_ref[...], far_ref[...]
    before = jnp.where(even, far, near)
    after = jnp.where(even, near, far)
    scales = [[] for _ in range(heights)]
    for b in range(cells // SUB):
        pieces = []
        for c in range(planes):
            pieces += [before[c, b * SUB :, :], own_ref[c], after[c, : (b + 1) * SUB, :]]
        pieces.append(jnp.zeros((depth - planes * window, width), jnp.bfloat16))
        part = jnp.dot(band_ref[...], jnp.concatenate(pieces, axis=0), preferred_element_type=jnp.float32)
        for h in range(heights):
            code, scale = coded(part[h * SUB : (h + 1) * SUB, :])
            read_ref[h, pl.ds(b * SUB, SUB), :] = code
            scales[h].append(scale)
    for h in range(heights):
        rest = jnp.ones((read_ref.shape[1] - cells - len(scales[h]), width), jnp.float32)
        read_ref[h, pl.ds(cells, read_ref.shape[1] - cells), :] = jnp.concatenate(scales[h] + [rest], axis=0).astype(jnp.bfloat16)


def span_kernel(gains_ref, read_ref, velocity_ref):
    blocks, height, width = read_ref.shape
    rows = velocity_ref.shape[1]
    cells = height - NOTES
    taps = gains_ref.shape[0]
    half = (taps - 1) // 2
    at = pl.multiple_of(pl.program_id(0) * rows, rows)
    chosen = lax.broadcasted_iota(jnp.int32, (NOTES, width), 0) == pl.program_id(0)
    parts = []
    for j in range(blocks):
        scale = jnp.sum(jnp.where(chosen, read_ref[j, pl.ds(cells, NOTES), :].astype(jnp.float32), 0.0), axis=0, keepdims=True)
        parts.append(decoded(read_ref[j, pl.ds(at, rows), :], scale))
    read = jnp.concatenate(parts, axis=1)
    shape = (rows, read.shape[1])
    total = jnp.zeros(shape, jnp.float32)
    for e in range(taps):
        gain = jnp.broadcast_to(gains_ref[e, 0:1, 0:1], shape)
        total = total + gain * (read if e == half else pltpu.roll(read, (half - e) % read.shape[1], 1))
    velocity_ref[0] = total


def tied(value, *after):
    return lax.optimization_barrier((value, *after))[0]


def local(wall_history, kernel_taps, span_gains):
    snaps, chans, cells, width = wall_history.shape
    taps = kernel_taps.shape[-1]
    planes = snaps * chans
    window = taps - 1 + SUB
    groups = lax.axis_size("ha")
    count = lax.axis_size("gx")
    depth = -(-planes * window // 128) * 128
    vmem, smem = pl.BlockSpec(memory_space=pltpu.VMEM), pl.BlockSpec(memory_space=pltpu.SMEM)
    params = pltpu.CompilerParams(vmem_limit_bytes=32 * 1024 * 1024)
    long = pl.CostEstimate(flops=40_000_000_000, bytes_accessed=1 << 16, transcendentals=0)

    rows = pl.pallas_call(
        row_kernel,
        out_shape=jax.ShapeDtypeStruct((groups, 1, depth), jnp.float32),
        in_specs=[vmem],
        out_specs=vmem,
        compiler_params=params,
    )(kernel_taps.reshape(snaps, chans, taps))
    own = tied(wall_history.reshape(planes, cells, width), rows)
    rows = lax.all_to_all(rows, "ha", 0, 0, tiled=True)
    far = lax.ppermute(own, "gx", [(i, (i - 1 if i % 2 == 0 else i + 1) % count) for i in range(count)])
    near = lax.ppermute(own, "gx", [(i, i ^ 1) for i in range(count)])
    wide = pl.pallas_call(
        gains_kernel,
        out_shape=jax.ShapeDtypeStruct((span_gains.shape[1], 8, 128), jnp.float32),
        in_specs=[vmem],
        out_specs=vmem,
        compiler_params=params,
        cost_estimate=long,
    )(span_gains)
    band = pl.pallas_call(
        band_kernel,
        out_shape=jax.ShapeDtypeStruct((groups * SUB, depth), jnp.bfloat16),
        in_specs=[vmem],
        out_specs=vmem,
        compiler_params=params,
    )(tied(rows, wide))
    even = (lax.axis_index("gx") % 2 == 0).astype(jnp.int32).reshape(1)
    read = pl.pallas_call(
        read_kernel,
        out_shape=jax.ShapeDtypeStruct((groups, cells + NOTES, width), jnp.bfloat16),
        in_specs=[smem] + [vmem] * 4,
        out_specs=vmem,
        compiler_params=params,
        cost_estimate=pl.CostEstimate(flops=2 * groups * cells * width * planes * window, bytes_accessed=2 << 20, transcendentals=0),
    )(even, band, own, near, far)
    read = lax.all_to_all(read, "ha", 0, 0, tiled=True)
    return pl.pallas_call(
        span_kernel,
        grid=(cells // SUB,),
        out_shape=jax.ShapeDtypeStruct((1, cells, groups * width), jnp.float32),
        in_specs=[vmem, vmem],
        out_specs=pl.BlockSpec((1, SUB, groups * width), lambda i: (0, i, 0)),
        compiler_params=params,
    )(wide, read)


def solution(mesh):
    in_specs = (P(None, None, "gx", "ha"), P("ha", None, None, None), P("ha", None))
    out_specs = P("ha", "gx", None)
    return jax.shard_map(local, mesh=mesh, in_specs=in_specs, out_specs=out_specs, check_vma=False)
```

time: 60.3 us -> 54.1 us (0.90)
  waiting for transfers between devices: 10.9 us -> 2.34 us
  blocking collectives: 20.8 us -> 22.9 us
  Pallas kernels: 4.66 us -> 5.65 us
    all_to_all x1, waiting for transfers between devices: 10.9 us -> 0.01 us  [local(): rows = lax.all_to_all(rows, 'ha', 0, 0, tiled=True)]
    ppermute x1, waiting for transfers between devices: 0.01 us -> 2.34 us  [local(): lax.ppermute(own, 'gx', [(i, (i - 1 if i % 2 == 0 else i + 1) % count) fo...]
    all_to_all x1, blocking collectives: 20.8 us -> 22.9 us  [local(): read = lax.all_to_all(read, 'ha', 0, 0, tiled=True)]
    unnamed x5 -> x6, local copies, waits for them, and re-layouts: 0.02 us -> 1.35 us
    pallas_call x2 -> x5, Pallas kernels: 4.66 us -> 5.65 us  [the longest x1 2.62 us: local(): pl.pallas_call(span_kernel, grid=(cells // SUB,), out_shape=jax.ShapeDtyp...]
    all_to_all x1, starting transfers between devices: 9.56 us -> 8.66 us  [local(): rows = lax.all_to_all(rows, 'ha', 0, 0, tiled=True)]
    reshape x2 -> x0, local copies, waits for them, and re-layouts: 0.81 us -> none  [the longest x1 0.72 us: local(): kernel_taps.astype(jnp.float32).reshape(planes, taps)]
    broadcast_in_dim x1 -> x0, local copies, waits for them, and re-layouts: 0.68 us -> none  [local(): jnp.broadcast_to(rows, (groups, depth))]
  transfers between devices with their start and end apart: 3 -> 3, of which waited for: 1 -> 1; matrix products, arithmetic and copies ran while one was open for 3% -> 0% of each run, Pallas kernels for 0% -> 1%
where the time goes in v2:
time: 54.1 us; the launch traced here: 53.7 us
  blocking collectives  22.9 us (42%)
  starting transfers between devices  21.5 us (40%)
  Pallas kernels  5.65 us (10%)
  waiting for transfers between devices  2.34 us (4%)
  local copies, waits for them, and re-layouts  1.35 us (2%)
    all_to_all x1, blocking collectives, local(): read = lax.all_to_all(read, 'ha', 0, 0, tiled=True)  22.9 us
    ppermute x1, starting transfers between devices, local(): lax.ppermute(own, 'gx', [(i, (i - 1 if i % 2 == 0 else i + 1) % count) fo...  10.9 us
    all_to_all x1, starting transfers between devices, local(): rows = lax.all_to_all(rows, 'ha', 0, 0, tiled=True)  8.66 us
    pallas_call x1, Pallas kernels, local(): pl.pallas_call(span_kernel, grid=(cells // SUB,), out_shape=jax.ShapeDtyp...  2.62 us
    ppermute x1, waiting for transfers between devices, local(): lax.ppermute(own, 'gx', [(i, (i - 1 if i % 2 == 0 else i + 1) % count) fo...  2.34 us
    ppermute x1, starting transfers between devices, local(): near = lax.ppermute(own, 'gx', [(i, i ^ 1) for i in range(count)])  1.92 us
    pallas_call x1, Pallas kernels, local(): pl.pallas_call(read_kernel, out_shape=jax.ShapeDtypeStruct((groups, cells...  1.8 us
    unnamed x6, local copies, waits for them, and re-layouts  1.35 us
  transfers between devices with their start and end apart: 3, of which 1 were waited for; matrix products, arithmetic and copies ran while one was open for 0% of the time, Pallas kernels for 1%

profile of v2, /device:TPU:8, one launch (start us, length us, event | category | flops | bytes accessed | tf_op | source)
XLA Modules:
  0.0 53.7 jit_solution(9188249415522184844)
XLA Ops:
  0.0 0.0 copy-start.1
  0.0 0.7 %copy-done.1 = bf16[1,3,3,257]{3,2,1,0:T(4,128)(2,1)S(1)} copy-done((bf16[1,3,3,257]{3,2,1,0:T(4,128)(2,1)S(1)}, bf16[1,3,3,257]{3,2,1,0:T(4,128)(2,1)}, u32[]{:S(2)}) %copy-start.1) | copy-done | bytes 4650
  0.7 0.7 %shard_map.38 = f32[8,1,2688]{2,1,0:T(1,128)} custom-call(bf16[3,3,257]{2,1,0:T(4,128)(2,1)S(1)} %bitcast.6), custom_call_target="tpu_custom_call" | custom-call | tf_op jit(solution)/shard_map/pallas_call | solution.py:120
  1.4 8.7 %all-to-all-start = ((f32[8,1,2688]{2,1,0:T(1,128)}), f32[8,1,2688]{2,1,0:T(1,128)S(1)}, u32[]{:S(2)}, u32[]{:S(2)}) async-start(f32[8,1,2688]{2,1,0:T(1,128)} %shard_map.38), calls=%async_computation | async-start | bytes 172032 | tf_op jit(solution)/shard_map/all_to_all | solution.py:128
  10.1 10.9 %collective-permute-start.1 = (bf16[9,128,128]{2,1,0:T(8,128)(2,1)}, bf16[9,128,128]{2,1,0:T(8,128)(2,1)S(1)}, u32[]{:S(2)}, u32[]{:S(2)}) collective-permute-start(bf16[9,128,128]{2,1,0:T(8,128)(2,1)} %bitcast.3), channel_id=1, source_target_pairs={{0,504},{8,16},{16,8},{24,32},{32,24},{40,48},{48,40},{56,64},{64,... | collective-permute-start | bytes 884744 | tf_op jit(solution)/shard_map/ppermute | solution.py:129
  21.0 1.9 %collective-permute-start = (bf16[9,128,128]{2,1,0:T(8,128)(2,1)}, bf16[9,128,128]{2,1,0:T(8,128)(2,1)S(1)}, u32[]{:S(2)}, u32[]{:S(2)}) collective-permute-start(bf16[9,128,128]{2,1,0:T(8,128)(2,1)} %bitcast.4), channel_id=1, source_target_pairs={{0,8},{8,0},{16,24},{24,16},{32,40},{40,32},{48,56},{56,48},{64,72... | collective-permute-start | bytes 884744 | tf_op jit(solution)/shard_map/ppermute | solution.py:130
  22.9 0.0 copy-start.2
  22.9 0.6 %copy-done.2 = f32[1,9]{1,0:T(1,128)S(1)} copy-done((f32[1,9]{1,0:T(1,128)S(1)}, f32[1,9]{1,0:T(1,128)}, u32[]{:S(2)}) %copy-start.2) | copy-done | bytes 60
  23.6 0.1 shard_map.37.gains_ref
  23.6 0.0 copy-start
  23.7 0.0 all-to-all-done.rows_ref
  23.7 0.4 shard_map.39.band_ref
  24.1 2.3 %collective-permute-done.1.far_ref = bf16[9,128,128]{2,1,0:T(8,128)(2,1)S(1)} collective-permute-done((bf16[9,128,128]{2,1,0:T(8,128)(2,1)}, bf16[9,128,128]{2,1,0:T(8,128)(2,1)S(1)}, u32[]{:S(2)}, u32[]{:S(2)}) %collective-permute-start.1) | collective-permute-done | bytes 294944 | tf_op jit(solution)/shard_map/ppermute | solution.py:129
  26.4 0.0 collective-permute-done.near_ref
  26.4 0.0 copy-done
  26.4 1.8 %shard_map.40 = bf16[8,144,128]{2,1,0:T(8,128)(2,1)S(1)} custom-call(s32[1]{0:T(128)} %bitcast.even_ref, bf16[256,2688]{1,0:T(8,128)(2,1)S(1)} %shard_map.39.band_ref, bf16[9,128,128]{2,1,0:T(8,128)(2,1)S(1)} %bitcast.5, bf16[9,128,128]{2,1,0:T(8,128)(2,1)S(1)} %collective-permute-done.near_ref, bf16[9,128,128]{2,1,0:T(8,128)(2,1)S(1)} %collective-permute-done.1.far_ref), custom_call_target="tpu_custom_call" | custom-call | flops 679477248 | bytes 2097152 | tf_op jit(solution)/shard_map/pallas_call | solution.py:147
  28.2 22.9 %all_to_all.10.read_ref = bf16[8,144,128]{2,1,0:T(8,128)(2,1)S(1)} all-to-all(bf16[8,144,128]{2,1,0:T(8,128)(2,1)S(1)} %shard_map.40), channel_id=1, replica_groups=mesh['gx'=64,'ha'=8] {'ha'}, dimensions={0} | all-to-all | bytes 589824 | tf_op jit(solution)/shard_map/all_to_all | solution.py:155
  51.1 2.6 %shard_map.41 = f32[1,128,1024]{2,1,0:T(8,128)} custom-call(f32[9,8,128]{2,1,0:T(8,128)S(1)} %shard_map.37.gains_ref, bf16[8,144,128]{2,1,0:T(8,128)(2,1)S(1)} %all_to_all.10.read_ref), custom_call_target="tpu_custom_call" | custom-call | tf_op jit(solution)/shard_map/pallas_call | solution.py:156
Async XLA Ops:
  0.0 0.7 %copy-start.1 = (bf16[1,3,3,257]{3,2,1,0:T(4,128)(2,1)S(1)}, bf16[1,3,3,257]{3,2,1,0:T(4,128)(2,1)}, u32[]{:S(2)}) copy-start(bf16[1,3,3,257]{3,2,1,0:T(4,128)(2,1)} %param.4) | copy-start | bytes 13882
  1.4 22.2 %all-to-all-start = ((f32[8,1,2688]{2,1,0:T(1,128)}), f32[8,1,2688]{2,1,0:T(1,128)S(1)}, u32[]{:S(2)}, u32[]{:S(2)}) async-start(f32[8,1,2688]{2,1,0:T(1,128)} %shard_map.38), calls=%async_computation | async-start | bytes 172032 | tf_op jit(solution)/shard_map/all_to_all | solution.py:128
  10.1 16.3 %collective-permute-start.1 = (bf16[9,128,128]{2,1,0:T(8,128)(2,1)}, bf16[9,128,128]{2,1,0:T(8,128)(2,1)S(1)}, u32[]{:S(2)}, u32[]{:S(2)}) collective-permute-start(bf16[9,128,128]{2,1,0:T(8,128)(2,1)} %bitcast.3), channel_id=1, source_target_pairs={{0,504},{8,16},{16,8},{24,32},{32,24},{40,48},{48,40},{56,64},{64,... | collective-permute-start | bytes 884744 | tf_op jit(solution)/shard_map/ppermute | solution.py:129
  21.0 5.4 %collective-permute-start = (bf16[9,128,128]{2,1,0:T(8,128)(2,1)}, bf16[9,128,128]{2,1,0:T(8,128)(2,1)S(1)}, u32[]{:S(2)}, u32[]{:S(2)}) collective-permute-start(bf16[9,128,128]{2,1,0:T(8,128)(2,1)} %bitcast.4), channel_id=1, source_target_pairs={{0,8},{8,0},{16,24},{24,16},{32,40},{40,32},{48,56},{56,48},{64,72... | collective-permute-start | bytes 884744 | tf_op jit(solution)/shard_map/ppermute | solution.py:130
  22.9 0.7 %copy-start.2 = (f32[1,9]{1,0:T(1,128)S(1)}, f32[1,9]{1,0:T(1,128)}, u32[]{:S(2)}) copy-start(f32[1,9]{1,0:T(1,128)} %gains_ref.1) | copy-start | bytes 112
  23.6 2.8 %copy-start = (bf16[3,3,128,128]{3,2,1,0:T(8,128)(2,1)S(1)}, bf16[3,3,128,128]{3,2,1,0:T(8,128)(2,1)}, u32[]{:S(2)}) copy-start(bf16[3,3,128,128]{3,2,1,0:T(8,128)(2,1)} %param.3) | copy-start | bytes 884740

commit v3 on v2

--- a/solution.py
+++ b/solution.py
@@ -13,28 +13,21 @@
 TINY = 1.2e-38
 
 
-def row_kernel(taps_ref, rows_ref):
-    groups, _, depth = rows_ref.shape
-    snaps, chans, taps = taps_ref.shape
-    pieces = []
-    for s in range(snaps):
-        for c in range(chans):
-            pieces += [taps_ref[s, c : c + 1, :].astype(jnp.float32), jnp.zeros((1, SUB - 1), jnp.float32)]
-    pieces.append(jnp.zeros((1, depth - snaps * chans * (taps + SUB - 1)), jnp.float32))
-    row = jnp.concatenate(pieces, axis=1)
-    for h in range(groups):
-        rows_ref[h] = row
-
-
 def gains_kernel(gains_ref, wide_ref):
     for e in range(gains_ref.shape[1]):
         wide_ref[e] = jnp.broadcast_to(gains_ref[0:1, e : e + 1], wide_ref.shape[1:])
 
 
-def band_kernel(rows_ref, band_ref):
-    heights, _, depth = rows_ref.shape
+def band_kernel(taps_ref, band_ref):
+    heights, snaps, chans, taps = taps_ref.shape
+    depth = band_ref.shape[1]
     for h in range(heights):
-        row = jnp.broadcast_to(rows_ref[h], (SUB, depth))
+        pieces = []
+        for s in range(snaps):
+            for c in range(chans):
+                pieces += [taps_ref[h, s, c : c + 1, :].astype(jnp.float32), jnp.zeros((1, SUB - 1), jnp.float32)]
+        pieces.append(jnp.zeros((1, depth - snaps * chans * (taps + SUB - 1)), jnp.float32))
+        row = jnp.broadcast_to(jnp.concatenate(pieces, axis=1), (SUB, depth))
         band_ref[pl.ds(h * SUB, SUB), :] = pltpu.roll(row, 0, 1, stride=1, stride_axis=0).astype(jnp.bfloat16)
 
 
@@ -65,16 +58,20 @@
     before = jnp.where(even, far, near)
     after = jnp.where(even, near, far)
     scales = [[] for _ in range(heights)]
-    for b in range(cells // SUB):
-        pieces = []
-        for c in range(planes):
-            pieces += [before[c, b * SUB :, :], own_ref[c], after[c, : (b + 1) * SUB, :]]
-        pieces.append(jnp.zeros((depth - planes * window, width), jnp.bfloat16))
-        part = jnp.dot(band_ref[...], jnp.concatenate(pieces, axis=0), preferred_element_type=jnp.float32)
+    for b in range(0, cells // SUB, 2):
+        spans = []
+        for at in (b * SUB, (b + 1) * SUB):
+            pieces = []
+            for c in range(planes):
+                pieces += [before[c, at:, :], own_ref[c], after[c, : at + SUB, :]]
+            pieces.append(jnp.zeros((depth - planes * window, width), jnp.bfloat16))
+            spans.append(jnp.concatenate(pieces, axis=0))
+        part = jnp.dot(band_ref[...], jnp.concatenate(spans, axis=1), preferred_element_type=jnp.float32)
         for h in range(heights):
-            code, scale = coded(part[h * SUB : (h + 1) * SUB, :])
-            read_ref[h, pl.ds(b * SUB, SUB), :] = code
-            scales[h].append(scale)
+            for k in range(2):
+                code, scale = coded(part[h * SUB : (h + 1) * SUB, k * width : (k + 1) * width])
+                read_ref[h, pl.ds((b + k) * SUB, SUB), :] = code
+                scales[h].append(scale)
     for h in range(heights):
         rest = jnp.ones((read_ref.shape[1] - cells - len(scales[h]), width), jnp.float32)
         read_ref[h, pl.ds(cells, read_ref.shape[1] - cells), :] = jnp.concatenate(scales[h] + [rest], axis=0).astype(jnp.bfloat16)
@@ -84,8 +81,6 @@
     blocks, height, width = read_ref.shape
     rows = velocity_ref.shape[1]
     cells = height - NOTES
-    taps = gains_ref.shape[0]
-    half = (taps - 1) // 2
     at = pl.multiple_of(pl.program_id(0) * rows, rows)
     chosen = lax.broadcasted_iota(jnp.int32, (NOTES, width), 0) == pl.program_id(0)
     parts = []
@@ -94,11 +89,19 @@
         parts.append(decoded(read_ref[j, pl.ds(at, rows), :], scale))
     read = jnp.concatenate(parts, axis=1)
     shape = (rows, read.shape[1])
-    total = jnp.zeros(shape, jnp.float32)
-    for e in range(taps):
-        gain = jnp.broadcast_to(gains_ref[e, 0:1, 0:1], shape)
-        total = total + gain * (read if e == half else pltpu.roll(read, (half - e) % read.shape[1], 1))
+    shifted = [pltpu.roll(read, 1, 1), read, pltpu.roll(read, shape[1] - 1, 1)]
+    total = 0.0
+    for k in range(3):
+        third = 0.0
+        for e in range(3):
+            third = third + jnp.broadcast_to(gains_ref[3 * k + e, 0:1, 0:1], shape) * shifted[e]
+        total = total + (third if k == 1 else pltpu.roll(third, (3 - 3 * k) % shape[1], 1))
     velocity_ref[0] = total
+
+
+def tap_groups(count, groups):
+    step = count // 2
+    return [[(g if h < groups // 2 else g ^ step) * groups + h for h in range(groups)] for g in range(count)]
 
 
 def tied(value, *after):
@@ -117,15 +120,9 @@
     params = pltpu.CompilerParams(vmem_limit_bytes=32 * 1024 * 1024)
     long = pl.CostEstimate(flops=40_000_000_000, bytes_accessed=1 << 16, transcendentals=0)
 
-    rows = pl.pallas_call(
-        row_kernel,
-        out_shape=jax.ShapeDtypeStruct((groups, 1, depth), jnp.float32),
-        in_specs=[vmem],
-        out_specs=vmem,
-        compiler_params=params,
-    )(kernel_taps.reshape(snaps, chans, taps))
+    rows = jnp.broadcast_to(kernel_taps, (groups, snaps, chans, taps))
     own = tied(wall_history.reshape(planes, cells, width), rows)
-    rows = lax.all_to_all(rows, "ha", 0, 0, tiled=True)
+    rows = lax.all_to_all(rows, ("gx", "ha"), 0, 0, tiled=True, axis_index_groups=tap_groups(count, groups))
     far = lax.ppermute(own, "gx", [(i, (i - 1 if i % 2 == 0 else i + 1) % count) for i in range(count)])
     near = lax.ppermute(own, "gx", [(i, i ^ 1) for i in range(count)])
     wide = pl.pallas_call(

time: 54.1 us -> 51.4 us (0.950)
  starting transfers between devices: 21.5 us -> 19.9 us
  Pallas kernels: 5.65 us -> 4.58 us
  waiting for transfers between devices: 2.34 us -> 1.68 us
  local copies, waits for them, and re-layouts: 1.35 us -> 2.01 us
    all_to_all x1, starting transfers between devices: 8.66 us -> 7.09 us  [local(): lax.all_to_all(rows, ('gx', 'ha'), 0, 0, tiled=True, axis_index_groups=ta...]
    broadcast_in_dim x0 -> x1, local copies, waits for them, and re-layouts: none -> 1.35 us  [local(): rows = jnp.broadcast_to(kernel_taps, (groups, snaps, chans, taps))]
    pallas_call x1 -> x0, Pallas kernels: 0.73 us -> none  [local(): pl.pallas_call(row_kernel, out_shape=jax.ShapeDtypeStruct((groups, 1, dep...]
    unnamed x6 -> x4, local copies, waits for them, and re-layouts: 1.35 us -> 0.65 us
    ppermute x1, waiting for transfers between devices: 2.34 us -> 1.67 us  [local(): lax.ppermute(own, 'gx', [(i, (i - 1 if i % 2 == 0 else i + 1) % count) fo...]
    pallas_call x1, Pallas kernels: 0.43 us -> 1.04 us  [local(): pl.pallas_call(band_kernel, out_shape=jax.ShapeDtypeStruct((groups * SUB,...]
    pallas_call x1, Pallas kernels: 1.8 us -> 1.22 us  [local(): pl.pallas_call(read_kernel, out_shape=jax.ShapeDtypeStruct((groups, cells...]
  transfers between devices with their start and end apart: 3 -> 3, of which waited for: 1 -> 1; matrix products, arithmetic and copies ran while one was open for 0% -> 0% of each run, Pallas kernels for 1% -> 2%
where the time goes in v3:
time: 51.4 us; the launch traced here: 51 us
  blocking collectives  22.8 us (44%)
  starting transfers between devices  19.9 us (39%)
  Pallas kernels  4.58 us (9%)
  local copies, waits for them, and re-layouts  2.01 us (4%)
  waiting for transfers between devices  1.68 us (3%)
    all_to_all x1, blocking collectives, local(): read = lax.all_to_all(read, 'ha', 0, 0, tiled=True)  22.8 us
    ppermute x1, starting transfers between devices, local(): lax.ppermute(own, 'gx', [(i, (i - 1 if i % 2 == 0 else i + 1) % count) fo...  10.9 us
    all_to_all x1, starting transfers between devices, local(): lax.all_to_all(rows, ('gx', 'ha'), 0, 0, tiled=True, axis_index_groups=ta...  7.09 us
    pallas_call x1, Pallas kernels, local(): pl.pallas_call(span_kernel, grid=(cells // SUB,), out_shape=jax.ShapeDtyp...  2.24 us
    ppermute x1, starting transfers between devices, local(): near = lax.ppermute(own, 'gx', [(i, i ^ 1) for i in range(count)])  1.92 us
    ppermute x1, waiting for transfers between devices, local(): lax.ppermute(own, 'gx', [(i, (i - 1 if i % 2 == 0 else i + 1) % count) fo...  1.67 us
    broadcast_in_dim x1, local copies, waits for them, and re-layouts, local(): rows = jnp.broadcast_to(kernel_taps, (groups, snaps, chans, taps))  1.35 us
    pallas_call x1, Pallas kernels, local(): pl.pallas_call(read_kernel, out_shape=jax.ShapeDtypeStruct((groups, cells...  1.22 us
  transfers between devices with their start and end apart: 3, of which 1 were waited for; matrix products, arithmetic and copies ran while one was open for 0% of the time, Pallas kernels for 2%

profile of v3, /device:TPU:8, one launch (start us, length us, event | category | flops | bytes accessed | tf_op | source)
XLA Modules:
  0.0 51.0 jit_solution(8459027538561836721)
XLA Ops:
  0.0 1.4 %broadcast_in_dim.8 = bf16[8,3,3,257]{3,2,1,0:T(4,128)(2,1)} broadcast(bf16[3,3,257]{2,1,0:T(4,128)(2,1)} %bitcast.6), dimensions={1,2,3} | broadcast | bytes 41634 | tf_op jit(solution)/shard_map/broadcast_in_dim | solution.py:123
  1.4 7.1 %all-to-all-start = ((bf16[8,3,3,257]{3,2,1,0:T(4,128)(2,1)}), bf16[8,3,3,257]{3,2,1,0:T(4,128)(2,1)S(1)}, u32[]{:S(2)}, u32[]{:S(2)}) async-start(bf16[8,3,3,257]{3,2,1,0:T(4,128)(2,1)} %broadcast_in_dim.8), calls=%async_computation | async-start | bytes 147456 | tf_op jit(solution)/shard_map/all_to_all | solution.py:125
  8.4 10.9 %collective-permute-start.1 = (bf16[9,128,128]{2,1,0:T(8,128)(2,1)}, bf16[9,128,128]{2,1,0:T(8,128)(2,1)S(1)}, u32[]{:S(2)}, u32[]{:S(2)}) collective-permute-start(bf16[9,128,128]{2,1,0:T(8,128)(2,1)} %bitcast.3), channel_id=1, source_target_pairs={{0,504},{8,16},{16,8},{24,32},{32,24},{40,48},{48,40},{56,64},{64,... | collective-permute-start | bytes 884744 | tf_op jit(solution)/shard_map/ppermute | solution.py:126
  19.3 1.9 %collective-permute-start = (bf16[9,128,128]{2,1,0:T(8,128)(2,1)}, bf16[9,128,128]{2,1,0:T(8,128)(2,1)S(1)}, u32[]{:S(2)}, u32[]{:S(2)}) collective-permute-start(bf16[9,128,128]{2,1,0:T(8,128)(2,1)} %bitcast.4), channel_id=1, source_target_pairs={{0,8},{8,0},{16,24},{24,16},{32,40},{40,32},{48,56},{56,48},{64,72... | collective-permute-start | bytes 884744 | tf_op jit(solution)/shard_map/ppermute | solution.py:127
  21.3 0.0 copy-start.1
  21.3 0.6 %copy-done.1 = f32[1,9]{1,0:T(1,128)S(1)} copy-done((f32[1,9]{1,0:T(1,128)S(1)}, f32[1,9]{1,0:T(1,128)}, u32[]{:S(2)}) %copy-start.1) | copy-done | bytes 60
  21.9 0.1 shard_map.37.gains_ref
  22.0 0.0 copy-start
  22.0 0.0 all-to-all-done.taps_ref
  22.0 1.0 %shard_map.38.band_ref = bf16[256,2688]{1,0:T(8,128)(2,1)S(1)} custom-call(bf16[8,3,3,257]{3,2,1,0:T(4,128)(2,1)S(1)} %all-to-all-done.taps_ref), custom_call_target="tpu_custom_call" | custom-call | tf_op jit(solution)/shard_map/pallas_call | solution.py:136
  23.1 1.7 %collective-permute-done.1.far_ref = bf16[9,128,128]{2,1,0:T(8,128)(2,1)S(1)} collective-permute-done((bf16[9,128,128]{2,1,0:T(8,128)(2,1)}, bf16[9,128,128]{2,1,0:T(8,128)(2,1)S(1)}, u32[]{:S(2)}, u32[]{:S(2)}) %collective-permute-start.1) | collective-permute-done | bytes 294944 | tf_op jit(solution)/shard_map/ppermute | solution.py:126
  24.7 0.0 collective-permute-done.near_ref
  24.7 0.0 copy-done
  24.7 1.2 %shard_map.39 = bf16[8,144,128]{2,1,0:T(8,128)(2,1)S(1)} custom-call(s32[1]{0:T(128)} %bitcast.even_ref, bf16[256,2688]{1,0:T(8,128)(2,1)S(1)} %shard_map.38.band_ref, bf16[9,128,128]{2,1,0:T(8,128)(2,1)S(1)} %bitcast.5, bf16[9,128,128]{2,1,0:T(8,128)(2,1)S(1)} %collective-permute-done.near_ref, bf16[9,128,128]{2,1,0:T(8,128)(2,1)S(1)} %collective-permute-done.1.far_ref), custom_call_target="tpu_custom_call" | custom-call | flops 679477248 | bytes 2097152 | tf_op jit(solution)/shard_map/pallas_call | solution.py:144
  26.0 22.8 %all_to_all.10.read_ref = bf16[8,144,128]{2,1,0:T(8,128)(2,1)S(1)} all-to-all(bf16[8,144,128]{2,1,0:T(8,128)(2,1)S(1)} %shard_map.39), channel_id=1, replica_groups=mesh['gx'=64,'ha'=8] {'ha'}, dimensions={0} | all-to-all | bytes 589824 | tf_op jit(solution)/shard_map/all_to_all | solution.py:152
  48.8 2.2 %shard_map.40 = f32[1,128,1024]{2,1,0:T(8,128)} custom-call(f32[9,8,128]{2,1,0:T(8,128)S(1)} %shard_map.37.gains_ref, bf16[8,144,128]{2,1,0:T(8,128)(2,1)S(1)} %all_to_all.10.read_ref), custom_call_target="tpu_custom_call" | custom-call | tf_op jit(solution)/shard_map/pallas_call | solution.py:153
Async XLA Ops:
  1.4 20.7 %all-to-all-start = ((bf16[8,3,3,257]{3,2,1,0:T(4,128)(2,1)}), bf16[8,3,3,257]{3,2,1,0:T(4,128)(2,1)S(1)}, u32[]{:S(2)}, u32[]{:S(2)}) async-start(bf16[8,3,3,257]{3,2,1,0:T(4,128)(2,1)} %broadcast_in_dim.8), calls=%async_computation | async-start | bytes 147456 | tf_op jit(solution)/shard_map/all_to_all | solution.py:125
  8.4 16.3 %collective-permute-start.1 = (bf16[9,128,128]{2,1,0:T(8,128)(2,1)}, bf16[9,128,128]{2,1,0:T(8,128)(2,1)S(1)}, u32[]{:S(2)}, u32[]{:S(2)}) collective-permute-start(bf16[9,128,128]{2,1,0:T(8,128)(2,1)} %bitcast.3), channel_id=1, source_target_pairs={{0,504},{8,16},{16,8},{24,32},{32,24},{40,48},{48,40},{56,64},{64,... | collective-permute-start | bytes 884744 | tf_op jit(solution)/shard_map/ppermute | solution.py:126
  19.3 5.4 %collective-permute-start = (bf16[9,128,128]{2,1,0:T(8,128)(2,1)}, bf16[9,128,128]{2,1,0:T(8,128)(2,1)S(1)}, u32[]{:S(2)}, u32[]{:S(2)}) collective-permute-start(bf16[9,128,128]{2,1,0:T(8,128)(2,1)} %bitcast.4), channel_id=1, source_target_pairs={{0,8},{8,0},{16,24},{24,16},{32,40},{40,32},{48,56},{56,48},{64,72... | collective-permute-start | bytes 884744 | tf_op jit(solution)/shard_map/ppermute | solution.py:127
  21.3 0.7 %copy-start.1 = (f32[1,9]{1,0:T(1,128)S(1)}, f32[1,9]{1,0:T(1,128)}, u32[]{:S(2)}) copy-start(f32[1,9]{1,0:T(1,128)} %gains_ref.1) | copy-start | bytes 112
  22.0 2.7 %copy-start = (bf16[3,3,128,128]{3,2,1,0:T(8,128)(2,1)S(1)}, bf16[3,3,128,128]{3,2,1,0:T(8,128)(2,1)}, u32[]{:S(2)}) copy-start(bf16[3,3,128,128]{3,2,1,0:T(8,128)(2,1)} %param.3) | copy-start | bytes 884740

commit v4 on v3

--- a/solution.py
+++ b/solution.py
@@ -7,10 +7,11 @@
 
 SUB = 32
 NOTES = 16
+STEP = 64
 LEVELS = 30719.0
 OFFSET = 120.0
 LOG2E = 1.4426950408889634
-TINY = 1.2e-38
+TINY = 2.0**-125
 
 
 def gains_kernel(gains_ref, wide_ref):
@@ -82,11 +83,16 @@
     rows = velocity_ref.shape[1]
     cells = height - NOTES
     at = pl.multiple_of(pl.program_id(0) * rows, rows)
-    chosen = lax.broadcasted_iota(jnp.int32, (NOTES, width), 0) == pl.program_id(0)
+    index = lax.broadcasted_iota(jnp.int32, (NOTES, width), 0)
     parts = []
     for j in range(blocks):
-        scale = jnp.sum(jnp.where(chosen, read_ref[j, pl.ds(cells, NOTES), :].astype(jnp.float32), 0.0), axis=0, keepdims=True)
-        parts.append(decoded(read_ref[j, pl.ds(at, rows), :], scale))
+        notes = read_ref[j, pl.ds(cells, NOTES), :].astype(jnp.float32)
+        pieces = []
+        for k in range(rows // SUB):
+            chosen = index == pl.program_id(0) * (rows // SUB) + k
+            scale = jnp.sum(jnp.where(chosen, notes, 0.0), axis=0, keepdims=True)
+            pieces.append(decoded(read_ref[j, pl.ds(at + k * SUB, SUB), :], scale))
+        parts.append(jnp.concatenate(pieces, axis=0))
     read = jnp.concatenate(parts, axis=1)
     shape = (rows, read.shape[1])
     shifted = [pltpu.roll(read, 1, 1), read, pltpu.roll(read, shape[1] - 1, 1)]
@@ -152,10 +158,10 @@
     read = lax.all_to_all(read, "ha", 0, 0, tiled=True)
     return pl.pallas_call(
         span_kernel,
-        grid=(cells // SUB,),
+        grid=(cells // STEP,),
         out_shape=jax.ShapeDtypeStruct((1, cells, groups * width), jnp.float32),
         in_specs=[vmem, vmem],
-        out_specs=pl.BlockSpec((1, SUB, groups * width), lambda i: (0, i, 0)),
+        out_specs=pl.BlockSpec((1, STEP, groups * width), lambda i: (0, i, 0)),
         compiler_params=params,
     )(wide, read)
 

time: 51.4 us -> 50.8 us (0.988)
  Pallas kernels: 4.58 us -> 4.03 us
    pallas_call x1, Pallas kernels: 2.24 us -> 1.69 us  [local(): pl.pallas_call(span_kernel, grid=(cells // STEP,), out_shape=jax.ShapeDty...]
where the time goes in v4:
time: 50.8 us; the launch traced here: 50.5 us
  blocking collectives  22.8 us (45%)
  starting transfers between devices  19.9 us (39%)
  Pallas kernels  4.03 us (8%)
  local copies, waits for them, and re-layouts  2.01 us (4%)
  waiting for transfers between devices  1.68 us (3%)
    all_to_all x1, blocking collectives, local(): read = lax.all_to_all(read, 'ha', 0, 0, tiled=True)  22.8 us
    ppermute x1, starting transfers between devices, local(): lax.ppermute(own, 'gx', [(i, (i - 1 if i % 2 == 0 else i + 1) % count) fo...  10.9 us
    all_to_all x1, starting transfers between devices, local(): lax.all_to_all(rows, ('gx', 'ha'), 0, 0, tiled=True, axis_index_groups=ta...  7.09 us
    ppermute x1, starting transfers between devices, local(): near = lax.ppermute(own, 'gx', [(i, i ^ 1) for i in range(count)])  1.92 us
    pallas_call x1, Pallas kernels, local(): pl.pallas_call(span_kernel, grid=(cells // STEP,), out_shape=jax.ShapeDty...  1.69 us
    ppermute x1, waiting for transfers between devices, local(): lax.ppermute(own, 'gx', [(i, (i - 1 if i % 2 == 0 else i + 1) % count) fo...  1.67 us
    broadcast_in_dim x1, local copies, waits for them, and re-layouts, local(): rows = jnp.broadcast_to(kernel_taps, (groups, snaps, chans, taps))  1.35 us
    pallas_call x1, Pallas kernels, local(): pl.pallas_call(read_kernel, out_shape=jax.ShapeDtypeStruct((groups, cells...  1.22 us
  transfers between devices with their start and end apart: 3, of which 1 were waited for; matrix products, arithmetic and copies ran while one was open for 0% of the time, Pallas kernels for 2%

profile of v4, /device:TPU:8, one launch (start us, length us, event | category | flops | bytes accessed | tf_op | source)
XLA Modules:
  0.0 50.5 jit_solution(15011835794033074627)
XLA Ops:
  0.0 1.4 %broadcast_in_dim.8 = bf16[8,3,3,257]{3,2,1,0:T(4,128)(2,1)} broadcast(bf16[3,3,257]{2,1,0:T(4,128)(2,1)} %bitcast.6), dimensions={1,2,3} | broadcast | bytes 41634 | tf_op jit(solution)/shard_map/broadcast_in_dim | solution.py:129
  1.4 7.1 %all-to-all-start = ((bf16[8,3,3,257]{3,2,1,0:T(4,128)(2,1)}), bf16[8,3,3,257]{3,2,1,0:T(4,128)(2,1)S(1)}, u32[]{:S(2)}, u32[]{:S(2)}) async-start(bf16[8,3,3,257]{3,2,1,0:T(4,128)(2,1)} %broadcast_in_dim.8), calls=%async_computation | async-start | bytes 147456 | tf_op jit(solution)/shard_map/all_to_all | solution.py:131
  8.4 10.9 %collective-permute-start.1 = (bf16[9,128,128]{2,1,0:T(8,128)(2,1)}, bf16[9,128,128]{2,1,0:T(8,128)(2,1)S(1)}, u32[]{:S(2)}, u32[]{:S(2)}) collective-permute-start(bf16[9,128,128]{2,1,0:T(8,128)(2,1)} %bitcast.3), channel_id=1, source_target_pairs={{0,504},{8,16},{16,8},{24,32},{32,24},{40,48},{48,40},{56,64},{64,... | collective-permute-start | bytes 884744 | tf_op jit(solution)/shard_map/ppermute | solution.py:132
  19.3 1.9 %collective-permute-start = (bf16[9,128,128]{2,1,0:T(8,128)(2,1)}, bf16[9,128,128]{2,1,0:T(8,128)(2,1)S(1)}, u32[]{:S(2)}, u32[]{:S(2)}) collective-permute-start(bf16[9,128,128]{2,1,0:T(8,128)(2,1)} %bitcast.4), channel_id=1, source_target_pairs={{0,8},{8,0},{16,24},{24,16},{32,40},{40,32},{48,56},{56,48},{64,72... | collective-permute-start | bytes 884744 | tf_op jit(solution)/shard_map/ppermute | solution.py:133
  21.3 0.0 copy-start.1
  21.3 0.6 %copy-done.1 = f32[1,9]{1,0:T(1,128)S(1)} copy-done((f32[1,9]{1,0:T(1,128)S(1)}, f32[1,9]{1,0:T(1,128)}, u32[]{:S(2)}) %copy-start.1) | copy-done | bytes 60
  21.9 0.1 shard_map.37.gains_ref
  22.0 0.0 copy-start
  22.0 0.0 all-to-all-done.taps_ref
  22.0 1.0 %shard_map.38.band_ref = bf16[256,2688]{1,0:T(8,128)(2,1)S(1)} custom-call(bf16[8,3,3,257]{3,2,1,0:T(4,128)(2,1)S(1)} %all-to-all-done.taps_ref), custom_call_target="tpu_custom_call" | custom-call | tf_op jit(solution)/shard_map/pallas_call | solution.py:142
  23.1 1.7 %collective-permute-done.1.far_ref = bf16[9,128,128]{2,1,0:T(8,128)(2,1)S(1)} collective-permute-done((bf16[9,128,128]{2,1,0:T(8,128)(2,1)}, bf16[9,128,128]{2,1,0:T(8,128)(2,1)S(1)}, u32[]{:S(2)}, u32[]{:S(2)}) %collective-permute-start.1) | collective-permute-done | bytes 294944 | tf_op jit(solution)/shard_map/ppermute | solution.py:132
  24.7 0.0 collective-permute-done.near_ref
  24.7 0.0 copy-done
  24.7 1.2 %shard_map.39 = bf16[8,144,128]{2,1,0:T(8,128)(2,1)S(1)} custom-call(s32[1]{0:T(128)} %bitcast.even_ref, bf16[256,2688]{1,0:T(8,128)(2,1)S(1)} %shard_map.38.band_ref, bf16[9,128,128]{2,1,0:T(8,128)(2,1)S(1)} %bitcast.5, bf16[9,128,128]{2,1,0:T(8,128)(2,1)S(1)} %collective-permute-done.near_ref, bf16[9,128,128]{2,1,0:T(8,128)(2,1)S(1)} %collective-permute-done.1.far_ref), custom_call_target="tpu_custom_call" | custom-call | flops 679477248 | bytes 2097152 | tf_op jit(solution)/shard_map/pallas_call | solution.py:150
  26.0 22.8 %all_to_all.10.read_ref = bf16[8,144,128]{2,1,0:T(8,128)(2,1)S(1)} all-to-all(bf16[8,144,128]{2,1,0:T(8,128)(2,1)S(1)} %shard_map.39), channel_id=1, replica_groups=mesh['gx'=64,'ha'=8] {'ha'}, dimensions={0} | all-to-all | bytes 589824 | tf_op jit(solution)/shard_map/all_to_all | solution.py:158
  48.8 1.7 %shard_map.40 = f32[1,128,1024]{2,1,0:T(8,128)} custom-call(f32[9,8,128]{2,1,0:T(8,128)S(1)} %shard_map.37.gains_ref, bf16[8,144,128]{2,1,0:T(8,128)(2,1)S(1)} %all_to_all.10.read_ref), custom_call_target="tpu_custom_call" | custom-call | tf_op jit(solution)/shard_map/pallas_call | solution.py:159
Async XLA Ops:
  1.4 20.7 %all-to-all-start = ((bf16[8,3,3,257]{3,2,1,0:T(4,128)(2,1)}), bf16[8,3,3,257]{3,2,1,0:T(4,128)(2,1)S(1)}, u32[]{:S(2)}, u32[]{:S(2)}) async-start(bf16[8,3,3,257]{3,2,1,0:T(4,128)(2,1)} %broadcast_in_dim.8), calls=%async_computation | async-start | bytes 147456 | tf_op jit(solution)/shard_map/all_to_all | solution.py:131
  8.4 16.3 %collective-permute-start.1 = (bf16[9,128,128]{2,1,0:T(8,128)(2,1)}, bf16[9,128,128]{2,1,0:T(8,128)(2,1)S(1)}, u32[]{:S(2)}, u32[]{:S(2)}) collective-permute-start(bf16[9,128,128]{2,1,0:T(8,128)(2,1)} %bitcast.3), channel_id=1, source_target_pairs={{0,504},{8,16},{16,8},{24,32},{32,24},{40,48},{48,40},{56,64},{64,... | collective-permute-start | bytes 884744 | tf_op jit(solution)/shard_map/ppermute | solution.py:132
  19.3 5.4 %collective-permute-start = (bf16[9,128,128]{2,1,0:T(8,128)(2,1)}, bf16[9,128,128]{2,1,0:T(8,128)(2,1)S(1)}, u32[]{:S(2)}, u32[]{:S(2)}) collective-permute-start(bf16[9,128,128]{2,1,0:T(8,128)(2,1)} %bitcast.4), channel_id=1, source_target_pairs={{0,8},{8,0},{16,24},{24,16},{32,40},{40,32},{48,56},{56,48},{64,72... | collective-permute-start | bytes 884744 | tf_op jit(solution)/shard_map/ppermute | solution.py:133
  21.3 0.7 %copy-start.1 = (f32[1,9]{1,0:T(1,128)S(1)}, f32[1,9]{1,0:T(1,128)}, u32[]{:S(2)}) copy-start(f32[1,9]{1,0:T(1,128)} %gains_ref.1) | copy-start | bytes 112
  22.0 2.7 %copy-start = (bf16[3,3,128,128]{3,2,1,0:T(8,128)(2,1)S(1)}, bf16[3,3,128,128]{3,2,1,0:T(8,128)(2,1)}, u32[]{:S(2)}) copy-start(bf16[3,3,128,128]{3,2,1,0:T(8,128)(2,1)} %param.3) | copy-start | bytes 884740

commit v5 on v4

--- a/solution.py
+++ b/solution.py
@@ -6,6 +6,7 @@
 from jax.sharding import PartitionSpec as P
 
 SUB = 32
+ORDER = (6, 7, 5, 4, 2, 3, 1, 0)
 NOTES = 16
 STEP = 64
 LEVELS = 30719.0
@@ -85,7 +86,7 @@
     at = pl.multiple_of(pl.program_id(0) * rows, rows)
     index = lax.broadcasted_iota(jnp.int32, (NOTES, width), 0)
     parts = []
-    for j in range(blocks):
+    for j in (ORDER.index(block) for block in range(blocks)):
         notes = read_ref[j, pl.ds(cells, NOTES), :].astype(jnp.float32)
         pieces = []
         for k in range(rows // SUB):
@@ -107,7 +108,7 @@
 
 def tap_groups(count, groups):
     step = count // 2
-    return [[(g if h < groups // 2 else g ^ step) * groups + h for h in range(groups)] for g in range(count)]
+    return [[(g if h < groups // 2 else g ^ step) * groups + h for h in ORDER] for g in range(count)]
 
 
 def tied(value, *after):
@@ -155,7 +156,7 @@
         compiler_params=params,
         cost_estimate=pl.CostEstimate(flops=2 * groups * cells * width * planes * window, bytes_accessed=2 << 20, transcendentals=0),
     )(even, band, own, near, far)
-    read = lax.all_to_all(read, "ha", 0, 0, tiled=True)
+    read = lax.all_to_all(read, "ha", 0, 0, tiled=True, axis_index_groups=[list(ORDER)])
     return pl.pallas_call(
         span_kernel,
         grid=(cells // STEP,),

time: 50.8 us -> 46.8 us (0.921)
  the two profiles are of different devices: /device:TPU:8 before, /device:TPU:4 now
where the time goes in v5:
time: 46.8 us; the launch traced here: 46.4 us
  starting transfers between devices  21.2 us (45%)
  blocking collectives  18.2 us (39%)
  Pallas kernels  4.03 us (9%)
  local copies, waits for them, and re-layouts  2.01 us (4%)
  waiting for transfers between devices  0.89 us (2%)
    all_to_all x1, blocking collectives, local(): lax.all_to_all(read, 'ha', 0, 0, tiled=True, axis_index_groups=[list(ORDE...  18.2 us
    all_to_all x1, starting transfers between devices, local(): lax.all_to_all(rows, ('gx', 'ha'), 0, 0, tiled=True, axis_index_groups=ta...  10.7 us
    ppermute x1, starting transfers between devices, local(): lax.ppermute(own, 'gx', [(i, (i - 1 if i % 2 == 0 else i + 1) % count) fo...  8.59 us
    ppermute x1, starting transfers between devices, local(): near = lax.ppermute(own, 'gx', [(i, i ^ 1) for i in range(count)])  1.92 us
    pallas_call x1, Pallas kernels, local(): pl.pallas_call(span_kernel, grid=(cells // STEP,), out_shape=jax.ShapeDty...  1.69 us
    broadcast_in_dim x1, local copies, waits for them, and re-layouts, local(): rows = jnp.broadcast_to(kernel_taps, (groups, snaps, chans, taps))  1.35 us
    pallas_call x1, Pallas kernels, local(): pl.pallas_call(read_kernel, out_shape=jax.ShapeDtypeStruct((groups, cells...  1.23 us
    pallas_call x1, Pallas kernels, local(): pl.pallas_call(band_kernel, out_shape=jax.ShapeDtypeStruct((groups * SUB,...  1.04 us
  transfers between devices with their start and end apart: 3, of which 1 were waited for; matrix products, arithmetic and copies ran while one was open for 0% of the time, Pallas kernels for 2%

profile of v5, /device:TPU:4, one launch (start us, length us, event | category | flops | bytes accessed | tf_op | source)
XLA Modules:
  0.0 46.4 jit_solution(2865698611013660516)
XLA Ops:
  0.0 1.4 %broadcast_in_dim.8 = bf16[8,3,3,257]{3,2,1,0:T(4,128)(2,1)} broadcast(bf16[3,3,257]{2,1,0:T(4,128)(2,1)} %bitcast.6), dimensions={1,2,3} | broadcast | bytes 41634 | tf_op jit(solution)/shard_map/broadcast_in_dim | solution.py:130
  1.4 10.7 %all-to-all-start = ((bf16[8,3,3,257]{3,2,1,0:T(4,128)(2,1)}), bf16[8,3,3,257]{3,2,1,0:T(4,128)(2,1)S(1)}, u32[]{:S(2)}, u32[]{:S(2)}) async-start(bf16[8,3,3,257]{3,2,1,0:T(4,128)(2,1)} %broadcast_in_dim.8), calls=%async_computation | async-start | bytes 147456 | tf_op jit(solution)/shard_map/all_to_all | solution.py:132
  12.1 8.6 %collective-permute-start.1 = (bf16[9,128,128]{2,1,0:T(8,128)(2,1)}, bf16[9,128,128]{2,1,0:T(8,128)(2,1)S(1)}, u32[]{:S(2)}, u32[]{:S(2)}) collective-permute-start(bf16[9,128,128]{2,1,0:T(8,128)(2,1)} %bitcast.3), channel_id=1, source_target_pairs={{0,504},{8,16},{16,8},{24,32},{32,24},{40,48},{48,40},{56,64},{64,... | collective-permute-start | bytes 884744 | tf_op jit(solution)/shard_map/ppermute | solution.py:133
  20.7 1.9 %collective-permute-start = (bf16[9,128,128]{2,1,0:T(8,128)(2,1)}, bf16[9,128,128]{2,1,0:T(8,128)(2,1)S(1)}, u32[]{:S(2)}, u32[]{:S(2)}) collective-permute-start(bf16[9,128,128]{2,1,0:T(8,128)(2,1)} %bitcast.4), channel_id=1, source_target_pairs={{0,8},{8,0},{16,24},{24,16},{32,40},{40,32},{48,56},{56,48},{64,72... | collective-permute-start | bytes 884744 | tf_op jit(solution)/shard_map/ppermute | solution.py:134
  22.6 0.0 copy-start.1
  22.6 0.6 %copy-done.1 = f32[1,9]{1,0:T(1,128)S(1)} copy-done((f32[1,9]{1,0:T(1,128)S(1)}, f32[1,9]{1,0:T(1,128)}, u32[]{:S(2)}) %copy-start.1) | copy-done | bytes 60
  23.3 0.1 shard_map.37.gains_ref
  23.3 0.0 copy-start
  23.3 0.0 all-to-all-done.taps_ref
  23.3 1.0 %shard_map.38.band_ref = bf16[256,2688]{1,0:T(8,128)(2,1)S(1)} custom-call(bf16[8,3,3,257]{3,2,1,0:T(4,128)(2,1)S(1)} %all-to-all-done.taps_ref), custom_call_target="tpu_custom_call" | custom-call | tf_op jit(solution)/shard_map/pallas_call | solution.py:143
  24.4 0.9 %collective-permute-done.1.far_ref = bf16[9,128,128]{2,1,0:T(8,128)(2,1)S(1)} collective-permute-done((bf16[9,128,128]{2,1,0:T(8,128)(2,1)}, bf16[9,128,128]{2,1,0:T(8,128)(2,1)S(1)}, u32[]{:S(2)}, u32[]{:S(2)}) %collective-permute-start.1) | collective-permute-done | bytes 294944 | tf_op jit(solution)/shard_map/ppermute | solution.py:133
  25.3 0.0 collective-permute-done.near_ref
  25.3 0.0 copy-done
  25.3 1.2 %shard_map.39 = bf16[8,144,128]{2,1,0:T(8,128)(2,1)S(1)} custom-call(s32[1]{0:T(128)} %bitcast.even_ref, bf16[256,2688]{1,0:T(8,128)(2,1)S(1)} %shard_map.38.band_ref, bf16[9,128,128]{2,1,0:T(8,128)(2,1)S(1)} %bitcast.5, bf16[9,128,128]{2,1,0:T(8,128)(2,1)S(1)} %collective-permute-done.near_ref, bf16[9,128,128]{2,1,0:T(8,128)(2,1)S(1)} %collective-permute-done.1.far_ref), custom_call_target="tpu_custom_call" | custom-call | flops 679477248 | bytes 2097152 | tf_op jit(solution)/shard_map/pallas_call | solution.py:151
  26.5 18.2 %all_to_all.10.read_ref = bf16[8,144,128]{2,1,0:T(8,128)(2,1)S(1)} all-to-all(bf16[8,144,128]{2,1,0:T(8,128)(2,1)S(1)} %shard_map.39), channel_id=1, replica_groups={{6,7,5,4,2,3,1,0},{14,15,13,12,10,11,9,8},{22,23,21,20,18,19,17,16},{30..., dimensions={0} | all-to-all | bytes 589824 | tf_op jit(solution)/shard_map/all_to_all | solution.py:159
  44.8 1.7 %shard_map.40 = f32[1,128,1024]{2,1,0:T(8,128)} custom-call(f32[9,8,128]{2,1,0:T(8,128)S(1)} %shard_map.37.gains_ref, bf16[8,144,128]{2,1,0:T(8,128)(2,1)S(1)} %all_to_all.10.read_ref), custom_call_target="tpu_custom_call" | custom-call | tf_op jit(solution)/shard_map/pallas_call | solution.py:160
Async XLA Ops:
  1.4 22.0 %all-to-all-start = ((bf16[8,3,3,257]{3,2,1,0:T(4,128)(2,1)}), bf16[8,3,3,257]{3,2,1,0:T(4,128)(2,1)S(1)}, u32[]{:S(2)}, u32[]{:S(2)}) async-start(bf16[8,3,3,257]{3,2,1,0:T(4,128)(2,1)} %broadcast_in_dim.8), calls=%async_computation | async-start | bytes 147456 | tf_op jit(solution)/shard_map/all_to_all | solution.py:132
  12.1 13.2 %collective-permute-start.1 = (bf16[9,128,128]{2,1,0:T(8,128)(2,1)}, bf16[9,128,128]{2,1,0:T(8,128)(2,1)S(1)}, u32[]{:S(2)}, u32[]{:S(2)}) collective-permute-start(bf16[9,128,128]{2,1,0:T(8,128)(2,1)} %bitcast.3), channel_id=1, source_target_pairs={{0,504},{8,16},{16,8},{24,32},{32,24},{40,48},{48,40},{56,64},{64,... | collective-permute-start | bytes 884744 | tf_op jit(solution)/shard_map/ppermute | solution.py:133
  20.7 4.6 %collective-permute-start = (bf16[9,128,128]{2,1,0:T(8,128)(2,1)}, bf16[9,128,128]{2,1,0:T(8,128)(2,1)S(1)}, u32[]{:S(2)}, u32[]{:S(2)}) collective-permute-start(bf16[9,128,128]{2,1,0:T(8,128)(2,1)} %bitcast.4), channel_id=1, source_target_pairs={{0,8},{8,0},{16,24},{24,16},{32,40},{40,32},{48,56},{56,48},{64,72... | collective-permute-start | bytes 884744 | tf_op jit(solution)/shard_map/ppermute | solution.py:134
  22.6 0.7 %copy-start.1 = (f32[1,9]{1,0:T(1,128)S(1)}, f32[1,9]{1,0:T(1,128)}, u32[]{:S(2)}) copy-start(f32[1,9]{1,0:T(1,128)} %gains_ref.1) | copy-start | bytes 112
  23.3 1.9 %copy-start = (bf16[3,3,128,128]{3,2,1,0:T(8,128)(2,1)S(1)}, bf16[3,3,128,128]{3,2,1,0:T(8,128)(2,1)}, u32[]{:S(2)}) copy-start(bf16[3,3,128,128]{3,2,1,0:T(8,128)(2,1)} %param.3) | copy-start | bytes 884740

commit v6 on v5

--- a/solution.py
+++ b/solution.py
@@ -6,7 +6,8 @@
 from jax.sharding import PartitionSpec as P
 
 SUB = 32
-ORDER = (6, 7, 5, 4, 2, 3, 1, 0)
+ORDER = (4, 5, 6, 7, 0, 1, 2, 3)
+TAP_ORDER = (6, 7, 5, 4, 2, 3, 1, 0)
 NOTES = 16
 STEP = 64
 LEVELS = 30719.0
@@ -30,7 +31,7 @@
                 pieces += [taps_ref[h, s, c : c + 1, :].astype(jnp.float32), jnp.zeros((1, SUB - 1), jnp.float32)]
         pieces.append(jnp.zeros((1, depth - snaps * chans * (taps + SUB - 1)), jnp.float32))
         row = jnp.broadcast_to(jnp.concatenate(pieces, axis=1), (SUB, depth))
-        band_ref[pl.ds(h * SUB, SUB), :] = pltpu.roll(row, 0, 1, stride=1, stride_axis=0).astype(jnp.bfloat16)
+        band_ref[pl.ds(ORDER.index(TAP_ORDER[h]) * SUB, SUB), :] = pltpu.roll(row, 0, 1, stride=1, stride_axis=0).astype(jnp.bfloat16)
 
 
 def coded(values):
@@ -108,7 +109,7 @@
 
 def tap_groups(count, groups):
     step = count // 2
-    return [[(g if h < groups // 2 else g ^ step) * groups + h for h in ORDER] for g in range(count)]
+    return [[(g if h < groups // 2 else g ^ step) * groups + h for h in TAP_ORDER] for g in range(count)]
 
 
 def tied(value, *after):

time: 46.8 us -> 46 us (0.983)
  the two profiles are of different devices: /device:TPU:4 before, /device:TPU:40 now
where the time goes in v6:
time: 46 us; the launch traced here: 45.7 us
  starting transfers between devices  19.1 us (42%)
  blocking collectives  18.8 us (41%)
  Pallas kernels  4.03 us (9%)
  local copies, waits for them, and re-layouts  2.01 us (4%)
  waiting for transfers between devices  1.68 us (4%)
    all_to_all x1, blocking collectives, local(): lax.all_to_all(read, 'ha', 0, 0, tiled=True, axis_index_groups=[list(ORDE...  18.8 us
    ppermute x1, starting transfers between devices, local(): lax.ppermute(own, 'gx', [(i, (i - 1 if i % 2 == 0 else i + 1) % count) fo...  10.9 us
    all_to_all x1, starting transfers between devices, local(): lax.all_to_all(rows, ('gx', 'ha'), 0, 0, tiled=True, axis_index_groups=ta...  6.29 us
    ppermute x1, starting transfers between devices, local(): near = lax.ppermute(own, 'gx', [(i, i ^ 1) for i in range(count)])  1.92 us
    pallas_call x1, Pallas kernels, local(): pl.pallas_call(span_kernel, grid=(cells // STEP,), out_shape=jax.ShapeDty...  1.69 us
    ppermute x1, waiting for transfers between devices, local(): lax.ppermute(own, 'gx', [(i, (i - 1 if i % 2 == 0 else i + 1) % count) fo...  1.67 us
    broadcast_in_dim x1, local copies, waits for them, and re-layouts, local(): rows = jnp.broadcast_to(kernel_taps, (groups, snaps, chans, taps))  1.35 us
    pallas_call x1, Pallas kernels, local(): pl.pallas_call(read_kernel, out_shape=jax.ShapeDtypeStruct((groups, cells...  1.22 us
  transfers between devices with their start and end apart: 3, of which 1 were waited for; matrix products, arithmetic and copies ran while one was open for 0% of the time, Pallas kernels for 2%

profile of v6, /device:TPU:40, one launch (start us, length us, event | category | flops | bytes accessed | tf_op | source)
XLA Modules:
  0.0 45.7 jit_solution(6801613598585452946)
XLA Ops:
  0.0 1.4 %broadcast_in_dim.8 = bf16[8,3,3,257]{3,2,1,0:T(4,128)(2,1)} broadcast(bf16[3,3,257]{2,1,0:T(4,128)(2,1)} %bitcast.6), dimensions={1,2,3} | broadcast | bytes 41634 | tf_op jit(solution)/shard_map/broadcast_in_dim | solution.py:131
  1.4 6.3 %all-to-all-start = ((bf16[8,3,3,257]{3,2,1,0:T(4,128)(2,1)}), bf16[8,3,3,257]{3,2,1,0:T(4,128)(2,1)S(1)}, u32[]{:S(2)}, u32[]{:S(2)}) async-start(bf16[8,3,3,257]{3,2,1,0:T(4,128)(2,1)} %broadcast_in_dim.8), calls=%async_computation | async-start | bytes 147456 | tf_op jit(solution)/shard_map/all_to_all | solution.py:133
  7.6 10.9 %collective-permute-start.1 = (bf16[9,128,128]{2,1,0:T(8,128)(2,1)}, bf16[9,128,128]{2,1,0:T(8,128)(2,1)S(1)}, u32[]{:S(2)}, u32[]{:S(2)}) collective-permute-start(bf16[9,128,128]{2,1,0:T(8,128)(2,1)} %bitcast.3), channel_id=1, source_target_pairs={{0,504},{8,16},{16,8},{24,32},{32,24},{40,48},{48,40},{56,64},{64,... | collective-permute-start | bytes 884744 | tf_op jit(solution)/shard_map/ppermute | solution.py:134
  18.5 1.9 %collective-permute-start = (bf16[9,128,128]{2,1,0:T(8,128)(2,1)}, bf16[9,128,128]{2,1,0:T(8,128)(2,1)S(1)}, u32[]{:S(2)}, u32[]{:S(2)}) collective-permute-start(bf16[9,128,128]{2,1,0:T(8,128)(2,1)} %bitcast.4), channel_id=1, source_target_pairs={{0,8},{8,0},{16,24},{24,16},{32,40},{40,32},{48,56},{56,48},{64,72... | collective-permute-start | bytes 884744 | tf_op jit(solution)/shard_map/ppermute | solution.py:135
  20.5 0.0 copy-start.1
  20.5 0.6 %copy-done.1 = f32[1,9]{1,0:T(1,128)S(1)} copy-done((f32[1,9]{1,0:T(1,128)S(1)}, f32[1,9]{1,0:T(1,128)}, u32[]{:S(2)}) %copy-start.1) | copy-done | bytes 60
  21.1 0.1 shard_map.37.gains_ref
  21.2 0.0 copy-start
  21.2 0.0 all-to-all-done.taps_ref
  21.2 1.0 %shard_map.38.band_ref = bf16[256,2688]{1,0:T(8,128)(2,1)S(1)} custom-call(bf16[8,3,3,257]{3,2,1,0:T(4,128)(2,1)S(1)} %all-to-all-done.taps_ref), custom_call_target="tpu_custom_call" | custom-call | tf_op jit(solution)/shard_map/pallas_call | solution.py:144
  22.3 1.7 %collective-permute-done.1.far_ref = bf16[9,128,128]{2,1,0:T(8,128)(2,1)S(1)} collective-permute-done((bf16[9,128,128]{2,1,0:T(8,128)(2,1)}, bf16[9,128,128]{2,1,0:T(8,128)(2,1)S(1)}, u32[]{:S(2)}, u32[]{:S(2)}) %collective-permute-start.1) | collective-permute-done | bytes 294944 | tf_op jit(solution)/shard_map/ppermute | solution.py:134
  23.9 0.0 collective-permute-done.near_ref
  23.9 0.0 copy-done
  23.9 1.2 %shard_map.39 = bf16[8,144,128]{2,1,0:T(8,128)(2,1)S(1)} custom-call(s32[1]{0:T(128)} %bitcast.even_ref, bf16[256,2688]{1,0:T(8,128)(2,1)S(1)} %shard_map.38.band_ref, bf16[9,128,128]{2,1,0:T(8,128)(2,1)S(1)} %bitcast.5, bf16[9,128,128]{2,1,0:T(8,128)(2,1)S(1)} %collective-permute-done.near_ref, bf16[9,128,128]{2,1,0:T(8,128)(2,1)S(1)} %collective-permute-done.1.far_ref), custom_call_target="tpu_custom_call" | custom-call | flops 679477248 | bytes 2097152 | tf_op jit(solution)/shard_map/pallas_call | solution.py:152
  25.2 18.8 %all_to_all.10.read_ref = bf16[8,144,128]{2,1,0:T(8,128)(2,1)S(1)} all-to-all(bf16[8,144,128]{2,1,0:T(8,128)(2,1)S(1)} %shard_map.39), channel_id=1, replica_groups={{4,5,6,7,0,1,2,3},{12,13,14,15,8,9,10,11},{20,21,22,23,16,17,18,19},{28..., dimensions={0} | all-to-all | bytes 589824 | tf_op jit(solution)/shard_map/all_to_all | solution.py:160
  44.0 1.7 %shard_map.40 = f32[1,128,1024]{2,1,0:T(8,128)} custom-call(f32[9,8,128]{2,1,0:T(8,128)S(1)} %shard_map.37.gains_ref, bf16[8,144,128]{2,1,0:T(8,128)(2,1)S(1)} %all_to_all.10.read_ref), custom_call_target="tpu_custom_call" | custom-call | tf_op jit(solution)/shard_map/pallas_call | solution.py:161
Async XLA Ops:
  1.4 19.9 %all-to-all-start = ((bf16[8,3,3,257]{3,2,1,0:T(4,128)(2,1)}), bf16[8,3,3,257]{3,2,1,0:T(4,128)(2,1)S(1)}, u32[]{:S(2)}, u32[]{:S(2)}) async-start(bf16[8,3,3,257]{3,2,1,0:T(4,128)(2,1)} %broadcast_in_dim.8), calls=%async_computation | async-start | bytes 147456 | tf_op jit(solution)/shard_map/all_to_all | solution.py:133
  7.6 16.3 %collective-permute-start.1 = (bf16[9,128,128]{2,1,0:T(8,128)(2,1)}, bf16[9,128,128]{2,1,0:T(8,128)(2,1)S(1)}, u32[]{:S(2)}, u32[]{:S(2)}) collective-permute-start(bf16[9,128,128]{2,1,0:T(8,128)(2,1)} %bitcast.3), channel_id=1, source_target_pairs={{0,504},{8,16},{16,8},{24,32},{32,24},{40,48},{48,40},{56,64},{64,... | collective-permute-start | bytes 884744 | tf_op jit(solution)/shard_map/ppermute | solution.py:134
  18.5 5.4 %collective-permute-start = (bf16[9,128,128]{2,1,0:T(8,128)(2,1)}, bf16[9,128,128]{2,1,0:T(8,128)(2,1)S(1)}, u32[]{:S(2)}, u32[]{:S(2)}) collective-permute-start(bf16[9,128,128]{2,1,0:T(8,128)(2,1)} %bitcast.4), channel_id=1, source_target_pairs={{0,8},{8,0},{16,24},{24,16},{32,40},{40,32},{48,56},{56,48},{64,72... | collective-permute-start | bytes 884744 | tf_op jit(solution)/shard_map/ppermute | solution.py:135
  20.5 0.7 %copy-start.1 = (f32[1,9]{1,0:T(1,128)S(1)}, f32[1,9]{1,0:T(1,128)}, u32[]{:S(2)}) copy-start(f32[1,9]{1,0:T(1,128)} %gains_ref.1) | copy-start | bytes 112
  21.2 2.7 %copy-start = (bf16[3,3,128,128]{3,2,1,0:T(8,128)(2,1)S(1)}, bf16[3,3,128,128]{3,2,1,0:T(8,128)(2,1)}, u32[]{:S(2)}) copy-start(bf16[3,3,128,128]{3,2,1,0:T(8,128)(2,1)} %param.3) | copy-start | bytes 884740

commit v7 on v6

--- a/solution.py
+++ b/solution.py
@@ -5,7 +5,7 @@
 from jax.experimental.pallas import tpu as pltpu
 from jax.sharding import PartitionSpec as P
 
-SUB = 32
+SUB = 16
 ORDER = (4, 5, 6, 7, 0, 1, 2, 3)
 TAP_ORDER = (6, 7, 5, 4, 2, 3, 1, 0)
 NOTES = 16

time: 46 us -> 45.5 us (0.989)
  the two profiles are of different devices: /device:TPU:40 before, /device:TPU:2 now
where the time goes in v7:
time: 45.5 us; the launch traced here: 45.2 us
  starting transfers between devices  22.3 us (49%)
  blocking collectives  15.9 us (35%)
  Pallas kernels  3.79 us (8%)
  waiting for transfers between devices  1.75 us (4%)
  local copies, waits for them, and re-layouts  1.36 us (3%)
    all_to_all x1, blocking collectives, local(): lax.all_to_all(read, 'ha', 0, 0, tiled=True, axis_index_groups=[list(ORDE...  15.9 us
    all_to_all x1, starting transfers between devices, local(): lax.all_to_all(rows, ('gx', 'ha'), 0, 0, tiled=True, axis_index_groups=ta...  11.7 us
    ppermute x1, starting transfers between devices, local(): lax.ppermute(own, 'gx', [(i, (i - 1 if i % 2 == 0 else i + 1) % count) fo...  8.73 us
    ppermute x1, starting transfers between devices, local(): near = lax.ppermute(own, 'gx', [(i, i ^ 1) for i in range(count)])  1.92 us
    ppermute x1, waiting for transfers between devices, local(): lax.ppermute(own, 'gx', [(i, (i - 1 if i % 2 == 0 else i + 1) % count) fo...  1.74 us
    pallas_call x1, Pallas kernels, local(): pl.pallas_call(span_kernel, grid=(cells // STEP,), out_shape=jax.ShapeDty...  1.71 us
    broadcast_in_dim x1, local copies, waits for them, and re-layouts, local(): rows = jnp.broadcast_to(kernel_taps, (groups, snaps, chans, taps))  1.35 us
    pallas_call x1, Pallas kernels, local(): pl.pallas_call(read_kernel, out_shape=jax.ShapeDtypeStruct((groups, cells...  1.18 us
  transfers between devices with their start and end apart: 3, of which 1 were waited for; matrix products, arithmetic and copies ran while one was open for 0% of the time, Pallas kernels for 2%

profile of v7, /device:TPU:2, one launch (start us, length us, event | category | flops | bytes accessed | tf_op | source)
XLA Modules:
  0.0 45.2 jit_solution(17296642290865188760)
XLA Ops:
  0.0 1.4 %broadcast_in_dim.8 = bf16[8,3,3,257]{3,2,1,0:T(4,128)(2,1)} broadcast(bf16[3,3,257]{2,1,0:T(4,128)(2,1)} %bitcast.6), dimensions={1,2,3} | broadcast | bytes 41634 | tf_op jit(solution)/shard_map/broadcast_in_dim | solution.py:131
  1.4 11.7 %all-to-all-start = ((bf16[8,3,3,257]{3,2,1,0:T(4,128)(2,1)}), bf16[8,3,3,257]{3,2,1,0:T(4,128)(2,1)S(1)}, u32[]{:S(2)}, u32[]{:S(2)}) async-start(bf16[8,3,3,257]{3,2,1,0:T(4,128)(2,1)} %broadcast_in_dim.8), calls=%async_computation | async-start | bytes 147456 | tf_op jit(solution)/shard_map/all_to_all | solution.py:133
  13.0 0.0 copy-start.1
  13.0 8.7 %collective-permute-start.1 = (bf16[9,128,128]{2,1,0:T(8,128)(2,1)}, bf16[9,128,128]{2,1,0:T(8,128)(2,1)S(1)}, u32[]{:S(2)}, u32[]{:S(2)}) collective-permute-start(bf16[9,128,128]{2,1,0:T(8,128)(2,1)} %bitcast.3), channel_id=1, source_target_pairs={{0,504},{8,16},{16,8},{24,32},{32,24},{40,48},{48,40},{56,64},{64,... | collective-permute-start | bytes 884744 | tf_op jit(solution)/shard_map/ppermute | solution.py:134
  21.7 1.9 %collective-permute-start = (bf16[9,128,128]{2,1,0:T(8,128)(2,1)}, bf16[9,128,128]{2,1,0:T(8,128)(2,1)S(1)}, u32[]{:S(2)}, u32[]{:S(2)}) collective-permute-start(bf16[9,128,128]{2,1,0:T(8,128)(2,1)} %bitcast.4), channel_id=1, source_target_pairs={{0,8},{8,0},{16,24},{24,16},{32,40},{40,32},{48,56},{56,48},{64,72... | collective-permute-start | bytes 884744 | tf_op jit(solution)/shard_map/ppermute | solution.py:135
  23.7 0.0 copy-done.1
  23.7 0.1 shard_map.37.gains_ref
  23.8 0.0 copy-start
  23.8 0.0 all-to-all-done.taps_ref
  23.8 0.8 %shard_map.38.band_ref = bf16[128,2560]{1,0:T(8,128)(2,1)S(1)} custom-call(bf16[8,3,3,257]{3,2,1,0:T(4,128)(2,1)S(1)} %all-to-all-done.taps_ref), custom_call_target="tpu_custom_call" | custom-call | tf_op jit(solution)/shard_map/pallas_call | solution.py:144
  24.6 1.7 %collective-permute-done.1.far_ref = bf16[9,128,128]{2,1,0:T(8,128)(2,1)S(1)} collective-permute-done((bf16[9,128,128]{2,1,0:T(8,128)(2,1)}, bf16[9,128,128]{2,1,0:T(8,128)(2,1)S(1)}, u32[]{:S(2)}, u32[]{:S(2)}) %collective-permute-start.1) | collective-permute-done | bytes 294944 | tf_op jit(solution)/shard_map/ppermute | solution.py:134
  26.4 0.0 collective-permute-done.near_ref
  26.4 0.0 copy-done
  26.4 1.2 %shard_map.39 = bf16[8,144,128]{2,1,0:T(8,128)(2,1)S(1)} custom-call(s32[1]{0:T(128)} %bitcast.even_ref, bf16[128,2560]{1,0:T(8,128)(2,1)S(1)} %shard_map.38.band_ref, bf16[9,128,128]{2,1,0:T(8,128)(2,1)S(1)} %bitcast.5, bf16[9,128,128]{2,1,0:T(8,128)(2,1)S(1)} %collective-permute-done.near_ref, bf16[9,128,128]{2,1,0:T(8,128)(2,1)S(1)} %collective-permute-done.1.far_ref), custom_call_target="tpu_custom_call" | custom-call | flops 641728512 | bytes 2097152 | tf_op jit(solution)/shard_map/pallas_call | solution.py:152
  27.5 15.9 %all_to_all.10.read_ref = bf16[8,144,128]{2,1,0:T(8,128)(2,1)S(1)} all-to-all(bf16[8,144,128]{2,1,0:T(8,128)(2,1)S(1)} %shard_map.39), channel_id=1, replica_groups={{4,5,6,7,0,1,2,3},{12,13,14,15,8,9,10,11},{20,21,22,23,16,17,18,19},{28..., dimensions={0} | all-to-all | bytes 589824 | tf_op jit(solution)/shard_map/all_to_all | solution.py:160
  43.5 1.7 %shard_map.40 = f32[1,128,1024]{2,1,0:T(8,128)} custom-call(f32[9,8,128]{2,1,0:T(8,128)S(1)} %shard_map.37.gains_ref, bf16[8,144,128]{2,1,0:T(8,128)(2,1)S(1)} %all_to_all.10.read_ref), custom_call_target="tpu_custom_call" | custom-call | tf_op jit(solution)/shard_map/pallas_call | solution.py:161
Async XLA Ops:
  1.4 22.4 %all-to-all-start = ((bf16[8,3,3,257]{3,2,1,0:T(4,128)(2,1)}), bf16[8,3,3,257]{3,2,1,0:T(4,128)(2,1)S(1)}, u32[]{:S(2)}, u32[]{:S(2)}) async-start(bf16[8,3,3,257]{3,2,1,0:T(4,128)(2,1)} %broadcast_in_dim.8), calls=%async_computation | async-start | bytes 147456 | tf_op jit(solution)/shard_map/all_to_all | solution.py:133
  13.0 10.7 %copy-start.1 = (f32[1,9]{1,0:T(1,128)S(1)}, f32[1,9]{1,0:T(1,128)}, u32[]{:S(2)}) copy-start(f32[1,9]{1,0:T(1,128)} %gains_ref.1) | copy-start | bytes 112
  13.0 13.3 %collective-permute-start.1 = (bf16[9,128,128]{2,1,0:T(8,128)(2,1)}, bf16[9,128,128]{2,1,0:T(8,128)(2,1)S(1)}, u32[]{:S(2)}, u32[]{:S(2)}) collective-permute-start(bf16[9,128,128]{2,1,0:T(8,128)(2,1)} %bitcast.3), channel_id=1, source_target_pairs={{0,504},{8,16},{16,8},{24,32},{32,24},{40,48},{48,40},{56,64},{64,... | collective-permute-start | bytes 884744 | tf_op jit(solution)/shard_map/ppermute | solution.py:134
  21.7 4.6 %collective-permute-start = (bf16[9,128,128]{2,1,0:T(8,128)(2,1)}, bf16[9,128,128]{2,1,0:T(8,128)(2,1)S(1)}, u32[]{:S(2)}, u32[]{:S(2)}) collective-permute-start(bf16[9,128,128]{2,1,0:T(8,128)(2,1)} %bitcast.4), channel_id=1, source_target_pairs={{0,8},{8,0},{16,24},{24,16},{32,40},{40,32},{48,56},{56,48},{64,72... | collective-permute-start | bytes 884744 | tf_op jit(solution)/shard_map/ppermute | solution.py:135
  23.8 2.6 %copy-start = (bf16[3,3,128,128]{3,2,1,0:T(8,128)(2,1)S(1)}, bf16[3,3,128,128]{3,2,1,0:T(8,128)(2,1)}, u32[]{:S(2)}) copy-start(bf16[3,3,128,128]{3,2,1,0:T(8,128)(2,1)} %param.3) | copy-start | bytes 884740

commit v8 on v7

--- a/solution.py
+++ b/solution.py
@@ -6,7 +6,7 @@
 from jax.sharding import PartitionSpec as P
 
 SUB = 16
-ORDER = (4, 5, 6, 7, 0, 1, 2, 3)
+ORDER = (4, 5, 6, 7, 3, 2, 1, 0)
 TAP_ORDER = (6, 7, 5, 4, 2, 3, 1, 0)
 NOTES = 16
 STEP = 64

time: 45.5 us -> 45.5 us (level)
  no operation moved by 1% of the time
where the time goes in v8:
time: 45.5 us; the launch traced here: 45.1 us
  starting transfers between devices  22.3 us (49%)
  blocking collectives  15.9 us (35%)
  Pallas kernels  3.79 us (8%)
  waiting for transfers between devices  1.75 us (4%)
  local copies, waits for them, and re-layouts  1.36 us (3%)
    all_to_all x1, blocking collectives, local(): lax.all_to_all(read, 'ha', 0, 0, tiled=True, axis_index_groups=[list(ORDE...  15.9 us
    all_to_all x1, starting transfers between devices, local(): lax.all_to_all(rows, ('gx', 'ha'), 0, 0, tiled=True, axis_index_groups=ta...  11.7 us
    ppermute x1, starting transfers between devices, local(): lax.ppermute(own, 'gx', [(i, (i - 1 if i % 2 == 0 else i + 1) % count) fo...  8.73 us
    ppermute x1, starting transfers between devices, local(): near = lax.ppermute(own, 'gx', [(i, i ^ 1) for i in range(count)])  1.92 us
    ppermute x1, waiting for transfers between devices, local(): lax.ppermute(own, 'gx', [(i, (i - 1 if i % 2 == 0 else i + 1) % count) fo...  1.74 us
    pallas_call x1, Pallas kernels, local(): pl.pallas_call(span_kernel, grid=(cells // STEP,), out_shape=jax.ShapeDty...  1.71 us
    broadcast_in_dim x1, local copies, waits for them, and re-layouts, local(): rows = jnp.broadcast_to(kernel_taps, (groups, snaps, chans, taps))  1.35 us
    pallas_call x1, Pallas kernels, local(): pl.pallas_call(read_kernel, out_shape=jax.ShapeDtypeStruct((groups, cells...  1.18 us
  transfers between devices with their start and end apart: 3, of which 1 were waited for; matrix products, arithmetic and copies ran while one was open for 0% of the time, Pallas kernels for 2%

profile of v8, /device:TPU:2, one launch (start us, length us, event | category | flops | bytes accessed | tf_op | source)
XLA Modules:
  0.0 45.1 jit_solution(7959498191582012251)
XLA Ops:
  0.0 1.4 %broadcast_in_dim.8 = bf16[8,3,3,257]{3,2,1,0:T(4,128)(2,1)} broadcast(bf16[3,3,257]{2,1,0:T(4,128)(2,1)} %bitcast.6), dimensions={1,2,3} | broadcast | bytes 41634 | tf_op jit(solution)/shard_map/broadcast_in_dim | solution.py:131
  1.4 11.7 %all-to-all-start = ((bf16[8,3,3,257]{3,2,1,0:T(4,128)(2,1)}), bf16[8,3,3,257]{3,2,1,0:T(4,128)(2,1)S(1)}, u32[]{:S(2)}, u32[]{:S(2)}) async-start(bf16[8,3,3,257]{3,2,1,0:T(4,128)(2,1)} %broadcast_in_dim.8), calls=%async_computation | async-start | bytes 147456 | tf_op jit(solution)/shard_map/all_to_all | solution.py:133
  13.0 0.0 copy-start.1
  13.0 8.7 %collective-permute-start.1 = (bf16[9,128,128]{2,1,0:T(8,128)(2,1)}, bf16[9,128,128]{2,1,0:T(8,128)(2,1)S(1)}, u32[]{:S(2)}, u32[]{:S(2)}) collective-permute-start(bf16[9,128,128]{2,1,0:T(8,128)(2,1)} %bitcast.3), channel_id=1, source_target_pairs={{0,504},{8,16},{16,8},{24,32},{32,24},{40,48},{48,40},{56,64},{64,... | collective-permute-start | bytes 884744 | tf_op jit(solution)/shard_map/ppermute | solution.py:134
  21.7 1.9 %collective-permute-start = (bf16[9,128,128]{2,1,0:T(8,128)(2,1)}, bf16[9,128,128]{2,1,0:T(8,128)(2,1)S(1)}, u32[]{:S(2)}, u32[]{:S(2)}) collective-permute-start(bf16[9,128,128]{2,1,0:T(8,128)(2,1)} %bitcast.4), channel_id=1, source_target_pairs={{0,8},{8,0},{16,24},{24,16},{32,40},{40,32},{48,56},{56,48},{64,72... | collective-permute-start | bytes 884744 | tf_op jit(solution)/shard_map/ppermute | solution.py:135
  23.7 0.0 copy-done.1
  23.7 0.1 shard_map.37.gains_ref
  23.8 0.0 copy-start
  23.8 0.0 all-to-all-done.taps_ref
  23.8 0.8 %shard_map.38.band_ref = bf16[128,2560]{1,0:T(8,128)(2,1)S(1)} custom-call(bf16[8,3,3,257]{3,2,1,0:T(4,128)(2,1)S(1)} %all-to-all-done.taps_ref), custom_call_target="tpu_custom_call" | custom-call | tf_op jit(solution)/shard_map/pallas_call | solution.py:144
  24.6 1.7 %collective-permute-done.1.far_ref = bf16[9,128,128]{2,1,0:T(8,128)(2,1)S(1)} collective-permute-done((bf16[9,128,128]{2,1,0:T(8,128)(2,1)}, bf16[9,128,128]{2,1,0:T(8,128)(2,1)S(1)}, u32[]{:S(2)}, u32[]{:S(2)}) %collective-permute-start.1) | collective-permute-done | bytes 294944 | tf_op jit(solution)/shard_map/ppermute | solution.py:134
  26.4 0.0 collective-permute-done.near_ref
  26.4 0.0 copy-done
  26.4 1.2 %shard_map.39 = bf16[8,144,128]{2,1,0:T(8,128)(2,1)S(1)} custom-call(s32[1]{0:T(128)} %bitcast.even_ref, bf16[128,2560]{1,0:T(8,128)(2,1)S(1)} %shard_map.38.band_ref, bf16[9,128,128]{2,1,0:T(8,128)(2,1)S(1)} %bitcast.5, bf16[9,128,128]{2,1,0:T(8,128)(2,1)S(1)} %collective-permute-done.near_ref, bf16[9,128,128]{2,1,0:T(8,128)(2,1)S(1)} %collective-permute-done.1.far_ref), custom_call_target="tpu_custom_call" | custom-call | flops 641728512 | bytes 2097152 | tf_op jit(solution)/shard_map/pallas_call | solution.py:152
  27.5 15.9 %all_to_all.10.read_ref = bf16[8,144,128]{2,1,0:T(8,128)(2,1)S(1)} all-to-all(bf16[8,144,128]{2,1,0:T(8,128)(2,1)S(1)} %shard_map.39), channel_id=1, replica_groups={{4,5,6,7,3,2,1,0},{12,13,14,15,11,10,9,8},{20,21,22,23,19,18,17,16},{28..., dimensions={0} | all-to-all | bytes 589824 | tf_op jit(solution)/shard_map/all_to_all | solution.py:160
  43.4 1.7 %shard_map.40 = f32[1,128,1024]{2,1,0:T(8,128)} custom-call(f32[9,8,128]{2,1,0:T(8,128)S(1)} %shard_map.37.gains_ref, bf16[8,144,128]{2,1,0:T(8,128)(2,1)S(1)} %all_to_all.10.read_ref), custom_call_target="tpu_custom_call" | custom-call | tf_op jit(solution)/shard_map/pallas_call | solution.py:161
Async XLA Ops:
  1.4 22.4 %all-to-all-start = ((bf16[8,3,3,257]{3,2,1,0:T(4,128)(2,1)}), bf16[8,3,3,257]{3,2,1,0:T(4,128)(2,1)S(1)}, u32[]{:S(2)}, u32[]{:S(2)}) async-start(bf16[8,3,3,257]{3,2,1,0:T(4,128)(2,1)} %broadcast_in_dim.8), calls=%async_computation | async-start | bytes 147456 | tf_op jit(solution)/shard_map/all_to_all | solution.py:133
  13.0 10.7 %copy-start.1 = (f32[1,9]{1,0:T(1,128)S(1)}, f32[1,9]{1,0:T(1,128)}, u32[]{:S(2)}) copy-start(f32[1,9]{1,0:T(1,128)} %gains_ref.1) | copy-start | bytes 112
  13.0 13.3 %collective-permute-start.1 = (bf16[9,128,128]{2,1,0:T(8,128)(2,1)}, bf16[9,128,128]{2,1,0:T(8,128)(2,1)S(1)}, u32[]{:S(2)}, u32[]{:S(2)}) collective-permute-start(bf16[9,128,128]{2,1,0:T(8,128)(2,1)} %bitcast.3), channel_id=1, source_target_pairs={{0,504},{8,16},{16,8},{24,32},{32,24},{40,48},{48,40},{56,64},{64,... | collective-permute-start | bytes 884744 | tf_op jit(solution)/shard_map/ppermute | solution.py:134
  21.7 4.6 %collective-permute-start = (bf16[9,128,128]{2,1,0:T(8,128)(2,1)}, bf16[9,128,128]{2,1,0:T(8,128)(2,1)S(1)}, u32[]{:S(2)}, u32[]{:S(2)}) collective-permute-start(bf16[9,128,128]{2,1,0:T(8,128)(2,1)} %bitcast.4), channel_id=1, source_target_pairs={{0,8},{8,0},{16,24},{24,16},{32,40},{40,32},{48,56},{56,48},{64,72... | collective-permute-start | bytes 884744 | tf_op jit(solution)/shard_map/ppermute | solution.py:135
  23.8 2.6 %copy-start = (bf16[3,3,128,128]{3,2,1,0:T(8,128)(2,1)S(1)}, bf16[3,3,128,128]{3,2,1,0:T(8,128)(2,1)}, u32[]{:S(2)}) copy-start(bf16[3,3,128,128]{3,2,1,0:T(8,128)(2,1)} %param.3) | copy-start | bytes 884740

commit v9 on v7

--- a/solution.py
+++ b/solution.py
@@ -9,7 +9,7 @@
 ORDER = (4, 5, 6, 7, 0, 1, 2, 3)
 TAP_ORDER = (6, 7, 5, 4, 2, 3, 1, 0)
 NOTES = 16
-STEP = 64
+STEP = 128
 LEVELS = 30719.0
 OFFSET = 120.0
 LOG2E = 1.4426950408889634
@@ -84,16 +84,13 @@
     blocks, height, width = read_ref.shape
     rows = velocity_ref.shape[1]
     cells = height - NOTES
-    at = pl.multiple_of(pl.program_id(0) * rows, rows)
-    index = lax.broadcasted_iota(jnp.int32, (NOTES, width), 0)
     parts = []
     for j in (ORDER.index(block) for block in range(blocks)):
         notes = read_ref[j, pl.ds(cells, NOTES), :].astype(jnp.float32)
         pieces = []
         for k in range(rows // SUB):
-            chosen = index == pl.program_id(0) * (rows // SUB) + k
-            scale = jnp.sum(jnp.where(chosen, notes, 0.0), axis=0, keepdims=True)
-            pieces.append(decoded(read_ref[j, pl.ds(at + k * SUB, SUB), :], scale))
+            scale = notes[k : k + 1]
+            pieces.append(decoded(read_ref[j, pl.ds(k * SUB, SUB), :], scale))
         parts.append(jnp.concatenate(pieces, axis=0))
     read = jnp.concatenate(parts, axis=1)
     shape = (rows, read.shape[1])

time: 45.5 us -> 45.5 us (level)
  no operation moved by 1% of the time
where the time goes in v9:
time: 45.5 us; the launch traced here: 45.2 us
  starting transfers between devices  22.3 us (49%)
  blocking collectives  15.9 us (35%)
  Pallas kernels  3.77 us (8%)
  waiting for transfers between devices  1.75 us (4%)
  local copies, waits for them, and re-layouts  1.36 us (3%)
    all_to_all x1, blocking collectives, local(): lax.all_to_all(read, 'ha', 0, 0, tiled=True, axis_index_groups=[list(ORDE...  15.9 us
    all_to_all x1, starting transfers between devices, local(): lax.all_to_all(rows, ('gx', 'ha'), 0, 0, tiled=True, axis_index_groups=ta...  11.7 us
    ppermute x1, starting transfers between devices, local(): lax.ppermute(own, 'gx', [(i, (i - 1 if i % 2 == 0 else i + 1) % count) fo...  8.73 us
    ppermute x1, starting transfers between devices, local(): near = lax.ppermute(own, 'gx', [(i, i ^ 1) for i in range(count)])  1.92 us
    ppermute x1, waiting for transfers between devices, local(): lax.ppermute(own, 'gx', [(i, (i - 1 if i % 2 == 0 else i + 1) % count) fo...  1.74 us
    pallas_call x1, Pallas kernels, local(): pl.pallas_call(span_kernel, grid=(cells // STEP,), out_shape=jax.ShapeDty...  1.69 us
    broadcast_in_dim x1, local copies, waits for them, and re-layouts, local(): rows = jnp.broadcast_to(kernel_taps, (groups, snaps, chans, taps))  1.35 us
    pallas_call x1, Pallas kernels, local(): pl.pallas_call(read_kernel, out_shape=jax.ShapeDtypeStruct((groups, cells...  1.18 us
  transfers between devices with their start and end apart: 3, of which 1 were waited for; matrix products, arithmetic and copies ran while one was open for 0% of the time, Pallas kernels for 2%

profile of v9, /device:TPU:2, one launch (start us, length us, event | category | flops | bytes accessed | tf_op | source)
XLA Modules:
  0.0 45.2 jit_solution(11916097376641437211)
XLA Ops:
  0.0 1.4 %broadcast_in_dim.8 = bf16[8,3,3,257]{3,2,1,0:T(4,128)(2,1)} broadcast(bf16[3,3,257]{2,1,0:T(4,128)(2,1)} %bitcast.6), dimensions={1,2,3} | broadcast | bytes 41634 | tf_op jit(solution)/shard_map/broadcast_in_dim | solution.py:128
  1.4 11.7 %all-to-all-start = ((bf16[8,3,3,257]{3,2,1,0:T(4,128)(2,1)}), bf16[8,3,3,257]{3,2,1,0:T(4,128)(2,1)S(1)}, u32[]{:S(2)}, u32[]{:S(2)}) async-start(bf16[8,3,3,257]{3,2,1,0:T(4,128)(2,1)} %broadcast_in_dim.8), calls=%async_computation | async-start | bytes 147456 | tf_op jit(solution)/shard_map/all_to_all | solution.py:130
  13.0 0.0 copy-start.1
  13.0 8.7 %collective-permute-start.1 = (bf16[9,128,128]{2,1,0:T(8,128)(2,1)}, bf16[9,128,128]{2,1,0:T(8,128)(2,1)S(1)}, u32[]{:S(2)}, u32[]{:S(2)}) collective-permute-start(bf16[9,128,128]{2,1,0:T(8,128)(2,1)} %bitcast.3), channel_id=1, source_target_pairs={{0,504},{8,16},{16,8},{24,32},{32,24},{40,48},{48,40},{56,64},{64,... | collective-permute-start | bytes 884744 | tf_op jit(solution)/shard_map/ppermute | solution.py:131
  21.7 1.9 %collective-permute-start = (bf16[9,128,128]{2,1,0:T(8,128)(2,1)}, bf16[9,128,128]{2,1,0:T(8,128)(2,1)S(1)}, u32[]{:S(2)}, u32[]{:S(2)}) collective-permute-start(bf16[9,128,128]{2,1,0:T(8,128)(2,1)} %bitcast.4), channel_id=1, source_target_pairs={{0,8},{8,0},{16,24},{24,16},{32,40},{40,32},{48,56},{56,48},{64,72... | collective-permute-start | bytes 884744 | tf_op jit(solution)/shard_map/ppermute | solution.py:132
  23.7 0.0 copy-done.1
  23.7 0.1 shard_map.37.gains_ref
  23.8 0.0 copy-start
  23.8 0.0 all-to-all-done.taps_ref
  23.8 0.8 %shard_map.38.band_ref = bf16[128,2560]{1,0:T(8,128)(2,1)S(1)} custom-call(bf16[8,3,3,257]{3,2,1,0:T(4,128)(2,1)S(1)} %all-to-all-done.taps_ref), custom_call_target="tpu_custom_call" | custom-call | tf_op jit(solution)/shard_map/pallas_call | solution.py:141
  24.6 1.7 %collective-permute-done.1.far_ref = bf16[9,128,128]{2,1,0:T(8,128)(2,1)S(1)} collective-permute-done((bf16[9,128,128]{2,1,0:T(8,128)(2,1)}, bf16[9,128,128]{2,1,0:T(8,128)(2,1)S(1)}, u32[]{:S(2)}, u32[]{:S(2)}) %collective-permute-start.1) | collective-permute-done | bytes 294944 | tf_op jit(solution)/shard_map/ppermute | solution.py:131
  26.4 0.0 collective-permute-done.near_ref
  26.4 0.0 copy-done
  26.4 1.2 %shard_map.39 = bf16[8,144,128]{2,1,0:T(8,128)(2,1)S(1)} custom-call(s32[1]{0:T(128)} %bitcast.even_ref, bf16[128,2560]{1,0:T(8,128)(2,1)S(1)} %shard_map.38.band_ref, bf16[9,128,128]{2,1,0:T(8,128)(2,1)S(1)} %bitcast.5, bf16[9,128,128]{2,1,0:T(8,128)(2,1)S(1)} %collective-permute-done.near_ref, bf16[9,128,128]{2,1,0:T(8,128)(2,1)S(1)} %collective-permute-done.1.far_ref), custom_call_target="tpu_custom_call" | custom-call | flops 641728512 | bytes 2097152 | tf_op jit(solution)/shard_map/pallas_call | solution.py:149
  27.5 15.9 %all_to_all.10.read_ref = bf16[8,144,128]{2,1,0:T(8,128)(2,1)S(1)} all-to-all(bf16[8,144,128]{2,1,0:T(8,128)(2,1)S(1)} %shard_map.39), channel_id=1, replica_groups={{4,5,6,7,0,1,2,3},{12,13,14,15,8,9,10,11},{20,21,22,23,16,17,18,19},{28..., dimensions={0} | all-to-all | bytes 589824 | tf_op jit(solution)/shard_map/all_to_all | solution.py:157
  43.5 1.7 %shard_map.40 = f32[1,128,1024]{2,1,0:T(8,128)} custom-call(f32[9,8,128]{2,1,0:T(8,128)S(1)} %shard_map.37.gains_ref, bf16[8,144,128]{2,1,0:T(8,128)(2,1)S(1)} %all_to_all.10.read_ref), custom_call_target="tpu_custom_call" | custom-call | tf_op jit(solution)/shard_map/pallas_call | solution.py:158
Async XLA Ops:
  1.4 22.4 %all-to-all-start = ((bf16[8,3,3,257]{3,2,1,0:T(4,128)(2,1)}), bf16[8,3,3,257]{3,2,1,0:T(4,128)(2,1)S(1)}, u32[]{:S(2)}, u32[]{:S(2)}) async-start(bf16[8,3,3,257]{3,2,1,0:T(4,128)(2,1)} %broadcast_in_dim.8), calls=%async_computation | async-start | bytes 147456 | tf_op jit(solution)/shard_map/all_to_all | solution.py:130
  13.0 10.7 %copy-start.1 = (f32[1,9]{1,0:T(1,128)S(1)}, f32[1,9]{1,0:T(1,128)}, u32[]{:S(2)}) copy-start(f32[1,9]{1,0:T(1,128)} %gains_ref.1) | copy-start | bytes 112
  13.0 13.3 %collective-permute-start.1 = (bf16[9,128,128]{2,1,0:T(8,128)(2,1)}, bf16[9,128,128]{2,1,0:T(8,128)(2,1)S(1)}, u32[]{:S(2)}, u32[]{:S(2)}) collective-permute-start(bf16[9,128,128]{2,1,0:T(8,128)(2,1)} %bitcast.3), channel_id=1, source_target_pairs={{0,504},{8,16},{16,8},{24,32},{32,24},{40,48},{48,40},{56,64},{64,... | collective-permute-start | bytes 884744 | tf_op jit(solution)/shard_map/ppermute | solution.py:131
  21.7 4.6 %collective-permute-start = (bf16[9,128,128]{2,1,0:T(8,128)(2,1)}, bf16[9,128,128]{2,1,0:T(8,128)(2,1)S(1)}, u32[]{:S(2)}, u32[]{:S(2)}) collective-permute-start(bf16[9,128,128]{2,1,0:T(8,128)(2,1)} %bitcast.4), channel_id=1, source_target_pairs={{0,8},{8,0},{16,24},{24,16},{32,40},{40,32},{48,56},{56,48},{64,72... | collective-permute-start | bytes 884744 | tf_op jit(solution)/shard_map/ppermute | solution.py:132
  23.8 2.6 %copy-start = (bf16[3,3,128,128]{3,2,1,0:T(8,128)(2,1)S(1)}, bf16[3,3,128,128]{3,2,1,0:T(8,128)(2,1)}, u32[]{:S(2)}) copy-start(bf16[3,3,128,128]{3,2,1,0:T(8,128)(2,1)} %param.3) | copy-start | bytes 884740
